TPU v7x, 256 devices: a whole 4x4x8 slice. The times are simulated.
256 devices in a mesh: tm: 32 (over x, z), inp: 4 (over y), integ: 2 (over core).
Axes of the slice: x: 4, y: 4, z: 8, core: 2. Of those that a mesh axis runs over, the one named last changes fastest.
Arguments:
- voltages: bfloat16 [256, 2, 256, 1024], P(('tm', 'integ'), None, None, 'inp'), may hold values from -6 to 6
- taps_coef: float32 [16, 256], replicated, may hold values from -1.5 to 1.5
- station_map: int32 [1024], replicated, may hold values from 0 to 1023, each once
- flags: int32 [1024], P('inp'), may hold values 0 or 1
Outputs:
- visibilities: float32 [256, 2, 1024, 1024], P(('tm', 'integ'), None, 'inp')
Inputs may be any that keep to these rules, and one draw needn't show every extreme that they name: station_map names every input once.
All inputs are finite; a program needn't handle non-finite values. No bound on the sum of `flags` on one device may be relied on, other than what follows from the above.
Results may differ from a plain program's by a relative error of at most 0.0036.
Values may be sent and summed in bfloat16 or wider, within the bound.
No kernel may reach another device: no remote copies, remote signals or barrier semaphores. Data moves between devices by JAX's collectives and lax.ppermute only.
A program may use at most 64 MiB of HBM per device.

v0:
```python
import math

import jax
import jax.numpy as jnp
from jax import lax
from jax.sharding import PartitionSpec as P


def shifted(block, axis, distance):
    devices = range(lax.axis_size(axis))
    route = [(i - distance, i) for i in devices if i - distance in devices]
    return lax.ppermute(block, axis, route)


def fourier_table(channels):
    grid = jnp.arange(channels, dtype=jnp.int32)
    phase_index = grid[:, None] * grid[None, :] % channels
    angles = phase_index.astype(jnp.float32) * (2.0 * math.pi / channels)
    output_scale = 1.0 / math.sqrt(channels)
    cosine = jnp.cos(angles) * output_scale
    sine = jnp.sin(angles) * output_scale
    return jnp.stack([jnp.stack([cosine, sine]), jnp.stack([-sine, cosine])])


def correlate(row_block, col_block, output_scale):
    real_part = jnp.einsum(
        "frci,frcj->cij", row_block, col_block, preferred_element_type=jnp.float32
    )
    reversed_order = jnp.stack([row_block[:, 1], -row_block[:, 0]], axis=1)
    imag_part = jnp.einsum(
        "frci,frcj->cij", reversed_order, col_block, preferred_element_type=jnp.float32
    )
    return jnp.stack([real_part, imag_part], axis=1) * output_scale


def local(voltages, taps_coef, station_map, flags):
    frames = voltages.shape[0]
    channels = voltages.shape[2]
    local_inputs = voltages.shape[3]
    tap_count = taps_coef.shape[0]
    shifts_needed = (tap_count - 1 + frames - 1) // frames
    earlier = [
        shifted(voltages, ("tm", "integ"), offset_frames)
        for offset_frames in range(shifts_needed, 0, -1)
    ]
    extended = jnp.concatenate(earlier + [voltages], axis=0)
    extended = extended[extended.shape[0] - (tap_count - 1 + frames) :]
    windowed = jnp.zeros(voltages.shape, jnp.float32)
    for tap_index in range(tap_count):
        windowed = windowed + taps_coef[tap_index][None, None, :, None] * extended[
            tap_index : tap_index + frames
        ].astype(jnp.float32)
    dft_table = fourier_table(channels)
    channel_spectra = jnp.einsum(
        "oicn,fina->foca", dft_table, windowed, precision=lax.Precision.HIGHEST
    )
    valid_blocks = (1 - flags).astype(jnp.float32)
    channel_spectra = (channel_spectra * valid_blocks[None, None, None, :]).astype(jnp.bfloat16)
    turned = lax.all_to_all(
        channel_spectra, ("tm", "integ"), split_axis=2, concat_axis=0, tiled=True
    )
    gathered = lax.all_gather(turned, "inp", axis=3, tiled=True)
    slot_index = lax.axis_index("inp") * local_inputs + jnp.arange(local_inputs, dtype=jnp.int32)
    row_inputs = jnp.take(station_map, slot_index, axis=0)
    row_block = jnp.take(gathered, row_inputs, axis=3)
    col_block = jnp.take(gathered, station_map, axis=3)
    output_scale = 1.0 / (frames * lax.axis_size("tm") * lax.axis_size("integ"))
    return correlate(row_block, col_block, output_scale)


def solution(mesh):
    return jax.shard_map(
        local,
        mesh=mesh,
        in_specs=(P(("tm", "integ"), None, None, "inp"), P(), P(), P("inp")),
        out_specs=P(("tm", "integ"), None, "inp", None),
        check_vma=False,
    )
```

profile of v0, /device:TPU:1, one launch (start us, length us, event | category | flops | bytes accessed | tf_op | source)
XLA Modules:
  0.0 278.3 jit_solution(12827542031596049773)
XLA Ops:
  6.5 5.9 %collective-permute-start = (bf16[4,2,256,256]{3,2,1,0:T(8,128)(2,1)}, bf16[4,2,256,256]{3,2,1,0:T(8,128)(2,1)S(1)}, u32[]{:S(2)}, u32[]{:S(2)}) collective-permute-start(bf16[4,2,256,256]{3,2,1,0:T(8,128)(2,1)} %param.4), channel_id=1, source_target_pairs={{0,16},{1,17},{8,24},{9,25},{16,32},{17,33},{24,40},{25,41},{32,48... | collective-permute-start | bytes 3145736 | tf_op jit(solution)/shard_map/ppermute | solution.py:12
  12.5 7.0 %collective-permute-start.1 = (bf16[4,2,256,256]{3,2,1,0:T(8,128)(2,1)}, bf16[4,2,256,256]{3,2,1,0:T(8,128)(2,1)S(1)}, u32[]{:S(2)}, u32[]{:S(2)}) collective-permute-start(bf16[4,2,256,256]{3,2,1,0:T(8,128)(2,1)} %param.4), channel_id=1, source_target_pairs={{0,9},{1,16},{8,17},{9,24},{16,25},{17,32},{24,33},{25,40},{32,41}... | collective-permute-start | bytes 3145736 | tf_op jit(solution)/shard_map/ppermute | solution.py:12
  19.4 1.9 collective-permute-start.3
  21.4 2.6 collective-permute-start.2
  24.0 1.0 fusion.95
  25.0 1.1 sine_multiply_fusion
  26.2 16.0 %collective-permute-done = bf16[4,2,256,256]{3,2,1,0:T(8,128)(2,1)S(1)} collective-permute-done((bf16[4,2,256,256]{3,2,1,0:T(8,128)(2,1)}, bf16[4,2,256,256]{3,2,1,0:T(8,128)(2,1)S(1)}, u32[]{:S(2)}, u32[]{:S(2)}) %collective-permute-start) | collective-permute-done | bytes 1048608 | tf_op jit(solution)/shard_map/ppermute | solution.py:12
  42.3 46.5 %collective-permute-done.1 = bf16[4,2,256,256]{3,2,1,0:T(8,128)(2,1)S(1)} collective-permute-done((bf16[4,2,256,256]{3,2,1,0:T(8,128)(2,1)}, bf16[4,2,256,256]{3,2,1,0:T(8,128)(2,1)S(1)}, u32[]{:S(2)}, u32[]{:S(2)}) %collective-permute-start.1) | collective-permute-done | bytes 1048608 | tf_op jit(solution)/shard_map/ppermute | solution.py:12
  89.0 36.6 %collective-permute-done.2 = bf16[4,2,256,256]{3,2,1,0:T(8,128)(2,1)S(1)} collective-permute-done((bf16[4,2,256,256]{3,2,1,0:T(8,128)(2,1)}, bf16[4,2,256,256]{3,2,1,0:T(8,128)(2,1)S(1)}, u32[]{:S(2)}, u32[]{:S(2)}) %collective-permute-start.2) | collective-permute-done | bytes 1048608 | tf_op jit(solution)/shard_map/ppermute | solution.py:12
  127.2 9.9 %fusion.52 = bf16[4,2,256,256]{2,3,1,0:T(8,128)(2,1)S(1)} fusion(bf16[4,2,256,256]{3,2,1,0:T(8,128)(2,1)S(1)} %copy-done.2, bf16[4,2,256,256]{3,2,1,0:T(8,128)(2,1)S(1)} %collective-permute-done.3, bf16[4,2,256,256]{3,2,1,0:T(8,128)(2,1)S(1)} %collective-permute-done.2, bf16[4,2,256,256]{3,2,1,0:T(8,128)(2,1)S(1)} %collective-permute-done.1, ...), kind=kOutput, calls=%fused_computation.58 | convolution fusion | flops 3247177728 | bytes 18891776 | tf_op jit(solution)/shard_map/oicn,fina->foca/dot_general | solution.py:54
  137.1 1.1 copy.16
  138.2 40.3 %all_to_all.18 = bf16[4,2,256,256]{3,1,0,2:T(2,128)(2,1)S(1)} all-to-all(bf16[4,2,256,256]{3,1,0,2:T(2,128)(2,1)S(1)} %copy.16), channel_id=1, replica_groups=mesh['tm'=32,'inp'=4,'integ'=2] {'tm','integ'}, dimensions={2} | all-to-all | bytes 2097152 | tf_op jit(solution)/shard_map/all_to_all | solution.py:59
  179.1 2.3 copy.19
  181.5 1.4 gather_fusion
  182.9 46.5 %all-gather.2.cloned.1.call-done = bf16[256,2,4,1024]{0,2,3,1:T(4,128)(2,1)} async-done(((bf16[256,2,4,256]{0,2,3,1:T(4,128)(2,1)}), bf16[256,2,4,1024]{0,2,3,1:T(4,128)(2,1)}) %all-gather.2.cloned.1.call-update) | async-done | bytes 4194320 | tf_op jit(solution)/shard_map/all_gather | solution.py:62
  229.4 13.2 %gather_fusion.2 = bf16[1024,256,2,4]{1,3,2,0:T(4,128)(2,1)} fusion(bf16[256,2,4,1024]{0,2,3,1:T(4,128)(2,1)} %all-gather.2.cloned.1.call-done, s32[1024]{0:T(1024)S(1)} %get-tuple-element.34), kind=kCustom, calls=%fused_computation.2 | custom fusion | bytes 8392704 | tf_op jit(solution)/shard_map/jit(_take)/gather | solution.py:66
  242.6 6.6 %select_bitcast_fusion = bf16[256,2,4,1024]{0,2,1,3:T(4,128)(2,1)} fusion(bf16[1024,256,2,4]{1,3,2,0:T(4,128)(2,1)} %gather_fusion.2, pred[1024]{0:T(1024)(128)(4,1)S(1)} %compare_and_fusion), kind=kLoop, calls=%fused_computation.4 | loop fusion | flops 2097152 | bytes 8389632 | tf_op jit(solution)/shard_map/jit(_take)/select_n | solution.py:66
  249.2 7.6 %copy.21 = bf16[256,2,4,1024]{3,0,1,2:T(8,128)(2,1)} copy(bf16[256,2,4,1024]{0,2,1,3:T(4,128)(2,1)} %select_bitcast_fusion) | data formatting | bytes 8388608 | tf_op jit(solution)/shard_map/jit(_take)/select_n | solution.py:66
  256.8 3.8 %gather_fusion.1 = bf16[256,256,2,4]{1,3,2,0:T(4,128)(2,1)S(1)} fusion(bf16[256,2,4,1024]{0,2,3,1:T(4,128)(2,1)} %all-gather.2.cloned.1.call-done, s32[1024]{0:T(1024)S(1)} %get-tuple-element.33), kind=kCustom, calls=%fused_computation.1 | custom fusion | bytes 2098176 | tf_op jit(solution)/shard_map/jit(_take)/gather | solution.py:65
  260.9 1.8 copy-done.1
  262.8 1.3 convolution_bitcast_fusion.1
  264.0 1.3 convolution_bitcast_fusion
  265.3 1.9 maximum_multiply_fusion
  267.2 4.2 %copy.23 = f32[4,2,256,1024]{3,2,1,0:T(8,128)} copy(f32[4,2,256,1024]{3,2,0,1:T(8,128)S(1)} %maximum_multiply_fusion) | data formatting | bytes 16777216 | tf_op jit(solution)/shard_map/mul | solution.py:33
  (29 shorter events, 2.9 us)
Async XLA Ops:
  6.5 19.6 %copy-start.4 = (s32[256]{0:T(256)S(1)}, s32[256]{0:T(256)}, u32[]{:S(2)}) copy-start(s32[256]{0:T(256)} %param.7) | copy-start | bytes 3076
  6.5 19.6 %copy-start.3 = (f32[16,256]{1,0:T(8,128)S(1)}, f32[16,256]{1,0:T(8,128)}, u32[]{:S(2)}) copy-start(f32[16,256]{1,0:T(8,128)} %param.5) | copy-start | bytes 49156
  6.5 222.9 %all-gather.2.cloned.1.call-start = ((), (), s32[]{:S(2)}) async-start(), calls=%async_computation.1 | async-start | bytes 5242880 | tf_op jit(solution)/shard_map/all_gather | solution.py:62
  6.5 35.6 %collective-permute-start = (bf16[4,2,256,256]{3,2,1,0:T(8,128)(2,1)}, bf16[4,2,256,256]{3,2,1,0:T(8,128)(2,1)S(1)}, u32[]{:S(2)}, u32[]{:S(2)}) collective-permute-start(bf16[4,2,256,256]{3,2,1,0:T(8,128)(2,1)} %param.4), channel_id=1, source_target_pairs={{0,16},{1,17},{8,24},{9,25},{16,32},{17,33},{24,40},{25,41},{32,48... | collective-permute-start | bytes 3145736 | tf_op jit(solution)/shard_map/ppermute | solution.py:12
  12.5 76.3 %collective-permute-start.1 = (bf16[4,2,256,256]{3,2,1,0:T(8,128)(2,1)}, bf16[4,2,256,256]{3,2,1,0:T(8,128)(2,1)S(1)}, u32[]{:S(2)}, u32[]{:S(2)}) collective-permute-start(bf16[4,2,256,256]{3,2,1,0:T(8,128)(2,1)} %param.4), channel_id=1, source_target_pairs={{0,9},{1,16},{8,17},{9,24},{16,25},{17,32},{24,33},{25,40},{32,41}... | collective-permute-start | bytes 3145736 | tf_op jit(solution)/shard_map/ppermute | solution.py:12
  19.4 106.5 %collective-permute-start.3 = (bf16[4,2,256,256]{3,2,1,0:T(8,128)(2,1)}, bf16[4,2,256,256]{3,2,1,0:T(8,128)(2,1)S(1)}, u32[]{:S(2)}, u32[]{:S(2)}) collective-permute-start(bf16[4,2,256,256]{3,2,1,0:T(8,128)(2,1)} %param.4), channel_id=1, source_target_pairs={{0,1},{1,8},{8,9},{9,16},{16,17},{17,24},{24,25},{25,32},{32,33},{... | collective-permute-start | bytes 3145736 | tf_op jit(solution)/shard_map/ppermute | solution.py:12
  21.4 104.3 %collective-permute-start.2 = (bf16[4,2,256,256]{3,2,1,0:T(8,128)(2,1)}, bf16[4,2,256,256]{3,2,1,0:T(8,128)(2,1)S(1)}, u32[]{:S(2)}, u32[]{:S(2)}) collective-permute-start(bf16[4,2,256,256]{3,2,1,0:T(8,128)(2,1)} %param.4), channel_id=1, source_target_pairs={{0,8},{1,9},{8,16},{9,17},{16,24},{17,25},{24,32},{25,33},{32,40},... | collective-permute-start | bytes 3145736 | tf_op jit(solution)/shard_map/ppermute | solution.py:12
  125.9 1.2 copy-start.2
  179.1 2.4 copy-start
  260.6 2.2 copy-start.1
Sparse Core Ops, SparseCore 0:
  181.6 47.8 all-gather.1
where the time goes:
time: 279 us; the launch traced here: 278 us
  waiting for transfers between devices  146 us (52%)
  blocking collectives  40.3 us (14%)
  local copies, waits for them, and re-layouts  37.8 us (14%)
  starting transfers between devices  17.4 us (6%)
  between operations  13.7 us (5%)
  matrix products  12.5 us (4%)
  other arithmetic  11 us (4%)
    ppermute x4, waiting for transfers between devices, shifted(): return lax.ppermute(block, axis, route)  99.1 us
    all_gather x1, waiting for transfers between devices, local(): gathered = lax.all_gather(turned, 'inp', axis=3, tiled=True)  46.5 us
    all_to_all x1, blocking collectives, local(): lax.all_to_all(channel_spectra, ('tm', 'integ'), split_axis=2, concat_axi...  40.3 us
    ppermute x4, starting transfers between devices, shifted(): return lax.ppermute(block, axis, route)  17.4 us
    gather x1, local copies, waits for them, and re-layouts, local(): col_block = jnp.take(gathered, station_map, axis=3)  13.2 us
    dot_general x1, matrix products, local(): jnp.einsum('oicn,fina->foca', dft_table, windowed, precision=lax.Precisio...  9.91 us
    select_n x1, local copies, waits for them, and re-layouts, local(): col_block = jnp.take(gathered, station_map, axis=3)  7.56 us
    select_n x1, other arithmetic, local(): col_block = jnp.take(gathered, station_map, axis=3)  6.63 us
  transfers between devices with their start and end apart: 5, of which 4 were waited for; matrix products, arithmetic and copies ran while one was open for 1% of the time, Pallas kernels for 0%

commit v1 on v0

v1 whole, which is shorter than its diff:
```python
import functools
import math

import jax
import jax.numpy as jnp
import ml_dtypes
import numpy as np
from jax import lax
from jax.experimental import pallas as pl
from jax.experimental.pallas import tpu as pltpu
from jax.sharding import PartitionSpec as P

TIME = ("tm", "integ")
BF16, F32 = jnp.bfloat16, jnp.float32
LANES = 128


def fourier_table(channels):
    grid = np.arange(channels)
    angles = (grid[:, None] * grid[None, :] % channels) * (2.0 * math.pi / channels)
    cosine = np.cos(angles) / math.sqrt(channels)
    sine = np.sin(angles) / math.sqrt(channels)
    table = np.block([[cosine, sine], [-sine, cosine]])
    high = table.astype(ml_dtypes.bfloat16)
    low = (table - high.astype(np.float64)).astype(ml_dtypes.bfloat16)
    return jnp.asarray(high), jnp.asarray(low)


def filter_kernel(
    taps, frames, parts, place, same, cross, left_same, left_cross, right_same, right_cross,
    coef, high, low, valid, *rest
):
    outs, (held, w_high, w_low, turned) = rest[:parts], rest[parts:]
    core, wraps = place[0], place[1]
    half = frames // 2
    samples = same.shape[2]
    first = core * half
    second = (1 - core) * half
    for start, mine, theirs in (
        (0, left_same, left_cross),
        (frames, same, cross),
        (2 * frames, right_same, right_cross),
    ):
        held[pl.ds(start + first, half)] = mine[...]
        held[pl.ds(start + second, half)] = theirs[...]

    @pl.when(wraps == 1)
    def _():
        held[frames : 2 * frames] = jnp.zeros((frames,) + same.shape[1:], BF16)

    rows = 16

    def one_block(block, carry):
        at = pl.multiple_of(block * rows, rows)
        factors = [coef[p, pl.ds(at, rows), :] for p in range(taps)]
        for part in range(2):
            sums = [None] * frames
            for j in range(2 * frames - taps + 1, 3 * frames):
                x = held[j, part, pl.ds(at, rows), :].astype(F32)
                for o in range(frames):
                    p = j - (2 * frames - taps + 1) - o
                    if 0 <= p < taps:
                        term = factors[p] * x
                        sums[o] = term if sums[o] is None else sums[o] + term
            for o in range(frames):
                top = sums[o].astype(BF16)
                rest_of = (sums[o] - top.astype(F32)).astype(BF16)
                lanes = slice((o % 2) * LANES, (o % 2 + 1) * LANES)
                to = pl.ds(pl.multiple_of(part * samples + at, rows), rows)
                w_high[o // 2, to, lanes] = top
                w_low[o // 2, to, lanes] = rest_of
        return carry

    lax.fori_loop(0, samples // rows, one_block, 0)

    keep = valid[...]
    channels = samples
    for pair in range(frames // 2):
        block = jnp.dot(high[...], w_high[pair], preferred_element_type=F32)
        block += jnp.dot(high[...], w_low[pair], preferred_element_type=F32)
        block += jnp.dot(low[...], w_high[pair], preferred_element_type=F32)
        for which in range(2):
            o = pair * 2 + which
            for part in range(2):
                piece = block[part * channels : (part + 1) * channels, which * LANES : (which + 1) * LANES]
                turned[pl.ds(part * frames + o, channels, stride=2 * frames), :] = piece * keep

    depth = 2 * frames
    dests, per_part = outs[0].shape[0], outs[0].shape[1]

    def one_dest(dest, carry):
        for n, out in enumerate(outs):
            at = pl.multiple_of((dest * parts + n) * per_part, per_part)
            out[dest] = turned[pl.ds(at, per_part), :].astype(BF16)
        return carry

    lax.fori_loop(0, dests, one_dest, 0)


def filter_bank(place, blocks, coef, high, low, valid, dests, parts):
    taps, samples, _ = coef.shape
    frames = 2 * blocks[0].shape[0]
    per_part = samples // dests // parts * 2 * frames
    vmem = pl.BlockSpec(memory_space=pltpu.VMEM)
    return pl.pallas_call(
        functools.partial(filter_kernel, taps, frames, parts),
        out_shape=[jax.ShapeDtypeStruct((dests, per_part, LANES), BF16)] * parts,
        in_specs=[pl.BlockSpec(memory_space=pltpu.SMEM)] + [vmem] * 10,
        out_specs=[vmem] * parts,
        scratch_shapes=[
            pltpu.VMEM((3 * frames, 2, samples, LANES), BF16),
            pltpu.VMEM((frames // 2, 2 * samples, 2 * LANES), BF16),
            pltpu.VMEM((frames // 2, 2 * samples, 2 * LANES), BF16),
            pltpu.VMEM((samples * 2 * frames, LANES), F32),
        ],
        compiler_params=pltpu.CompilerParams(vmem_limit_bytes=48 * 2**20),
        name="filter_bank",
    )(place, *blocks, coef, high, low, valid)


def correlate_kernel(scale, cores, part_rows, row_at, *refs):
    blocks, (pick, pick_rows, *_), out = refs[:4], refs[4:-1], refs[-1]
    channel = pl.program_id(0)
    at = pl.multiple_of(channel * part_rows, part_rows)
    columns = []
    for block in blocks:
        for core in range(cores):
            tile = block[:, core, pl.ds(at, part_rows), :]
            columns.append(tile.reshape(-1, LANES))
    gathered = jnp.concatenate(columns, axis=1)
    lhs = lax.dot_general(
        pick_rows[...], gathered, (((1,), (1,)), ((), ())), preferred_element_type=F32
    ).astype(BF16)
    ordered = jnp.dot(gathered, pick[...], preferred_element_type=F32)
    half = part_rows // 2
    split = ordered.reshape(-1, 2, half, ordered.shape[1])
    direct = ordered.astype(BF16)
    flipped = jnp.stack([-split[:, 1], split[:, 0]], axis=1).reshape(ordered.shape).astype(BF16)
    out[0, 0] = jnp.dot(lhs, direct, preferred_element_type=F32) * scale
    out[0, 1] = jnp.dot(lhs, flipped, preferred_element_type=F32) * scale


def correlate(blocks, pick, pick_rows, scale, part_rows, shape, first, so_far):
    count = blocks[0].shape[2] // part_rows
    whole = lambda a: pl.BlockSpec(a.shape, lambda i: (0,) * a.ndim)
    operands = [*blocks, pick, pick_rows]
    specs = [whole(a) for a in operands]
    aliases = {}
    if so_far is not None:
        operands.append(so_far)
        specs.append(pl.BlockSpec(memory_space=pl.ANY))
        aliases = {len(operands) - 1: 0}
    body = functools.partial(correlate_kernel, scale, blocks[0].shape[1], part_rows, None)
    return pl.pallas_call(
        body,
        grid=(count,),
        out_shape=jax.ShapeDtypeStruct(shape, F32),
        in_specs=specs,
        out_specs=pl.BlockSpec((1,) + shape[1:], lambda i: (first + i, 0, 0, 0)),
        input_output_aliases=aliases,
        compiler_params=pltpu.CompilerParams(vmem_limit_bytes=48 * 2**20),
        name="correlate",
    )(*operands)


def local(voltages, taps_coef, station_map, flags):
    frames, _, samples, width = voltages.shape
    chips, cores, rows = lax.axis_size("tm"), lax.axis_size("integ"), lax.axis_size("inp")
    chip, core, row = lax.axis_index("tm"), lax.axis_index("integ"), lax.axis_index("inp")
    index = lambda t, c: t * cores + c
    same = lax.dynamic_slice_in_dim(voltages, core * LANES, LANES, axis=3)
    cross = lax.dynamic_slice_in_dim(voltages, (1 - core) * LANES, LANES, axis=3)

    def route(step, swap):
        pairs = []
        for t in range(chips):
            source = t - step
            if step == 1 and t in (0, chips - 1):
                continue
            for c in range(cores):
                pairs.append((index(source % chips, c ^ swap), index(t, c)))
        return pairs

    with jax.named_scope("halo"):
        right_cross = lax.ppermute(cross, TIME, route(-1, 1))
        left_cross = lax.ppermute(cross, TIME, route(1, 1))
        right_same = lax.ppermute(same, TIME, route(-1, 0))
        left_same = lax.ppermute(same, TIME, route(1, 0))
        own_cross = lax.ppermute(cross, TIME, route(0, 1))
    coef = jnp.broadcast_to(taps_coef[:, :, None], taps_coef.shape + (LANES,))
    high, low = fourier_table(samples)
    valid = lax.dynamic_slice_in_dim((1 - flags).astype(F32), core * LANES, LANES)[None, :]
    place = jnp.stack([core, (chip == chips - 1).astype(jnp.int32)]).astype(jnp.int32)
    dests, parts = chips * cores, 2
    with jax.named_scope("filter"):
        spectra = filter_bank(
            place,
            (same, own_cross, left_same, left_cross, right_same, right_cross),
            coef, high, low, valid, dests, parts,
        )

    inputs = width * rows
    order = jnp.arange(inputs, dtype=jnp.int32)
    held_input = (row + order // width) % rows * width + order % width
    pick = (held_input[:, None] == station_map[None, :]).astype(BF16)
    own_slots = lax.dynamic_slice_in_dim(station_map, row * width, width)
    pick_rows = (own_slots[:, None] == held_input[None, :]).astype(BF16)

    turned, gathered = [], []
    for spectrum in spectra:
        with jax.named_scope("exchange"):
            turned.append(lax.all_to_all(spectrum, TIME, 0, 0, tiled=True))
    shape = (samples // dests, 2, width, inputs)
    scale = 1.0 / (frames * dests)
    out = None
    per_part = shape[0] // parts
    for n, block in enumerate(turned):
        with jax.named_scope("gather"):
            blocks = [block] + [
                lax.ppermute(block, "inp", [((i + d) % rows, i) for i in range(rows)]) for d in range(1, rows)
            ]
        blocks = [b.reshape(chips, cores, -1, LANES) for b in blocks]
        with jax.named_scope("correlate"):
            out = correlate(blocks, pick, pick_rows, scale, 4 * frames, shape, n * per_part, out)
    return out


def solution(mesh):
    return jax.shard_map(
        local,
        mesh=mesh,
        in_specs=(P(("tm", "integ"), None, None, "inp"), P(), P(), P("inp")),
        out_specs=P(("tm", "integ"), None, "inp", None),
        check_vma=False,
    )
```

time: 279 us -> 135 us (0.48)
  waiting for transfers between devices: 146 us -> 51.1 us
  local copies, waits for them, and re-layouts: 37.8 us -> 4.98 us
  Pallas kernels: 0 us -> 20.9 us
  blocking collectives: 40.3 us -> 25.4 us
  starting transfers between devices: 17.4 us -> 31.1 us
  between operations: 13.7 us -> 0.07 us
  matrix products: 12.5 us -> 0 us
  other arithmetic: 11 us -> 1.33 us
    ppermute x4 -> x11, waiting for transfers between devices: 99.1 us -> 38.8 us  [the longest x6 20.9 us: local(): lax.ppermute(block, 'inp', [((i + d) % rows, i) for i in range(rows)])]
    all_gather x1 -> x0, waiting for transfers between devices: 46.5 us -> none  [local(): gathered = lax.all_gather(turned, 'inp', axis=3, tiled=True)]
    pallas_call x0 -> x3, Pallas kernels: none -> 20.9 us  [the longest x2 12.3 us: correlate(): pl.pallas_call(body, grid=(count,), out_shape=jax.ShapeDtypeStruct(shape,...]
    gather x3 -> x0, local copies, waits for them, and re-layouts: 18.3 us -> none  [the longest x1 13.2 us: local(): col_block = jnp.take(gathered, station_map, axis=3)]
    all_to_all x1, blocking collectives: 40.3 us -> 25.4 us  [local(): turned.append(lax.all_to_all(spectrum, TIME, 0, 0, tiled=True))]
    dot_general x3 -> x0, matrix products: 12.5 us -> none  [the longest x1 9.91 us: local(): jnp.einsum('oicn,fina->foca', dft_table, windowed, precision=lax.Precisio...]
    all_to_all x0 -> x1, waiting for transfers between devices: none -> 12.3 us  [local(): turned.append(lax.all_to_all(spectrum, TIME, 0, 0, tiled=True))]
    select_n x1 -> x0, local copies, waits for them, and re-layouts: 7.56 us -> none  [local(): col_block = jnp.take(gathered, station_map, axis=3)]
  transfers between devices with their start and end apart: 5 -> 12, of which waited for: 4 -> 8; matrix products, arithmetic and copies ran while one was open for 1% -> 1% of each run, Pallas kernels for 0% -> 4%
where the time goes in v1:
time: 135 us
  waiting for transfers between devices  51.1 us (38%)
  starting transfers between devices  31.1 us (23%)
  blocking collectives  25.4 us (19%)
  Pallas kernels  20.9 us (15%)
  local copies, waits for them, and re-layouts  4.98 us (4%)
    all_to_all x1, blocking collectives, local(): turned.append(lax.all_to_all(spectrum, TIME, 0, 0, tiled=True))  25.4 us
    ppermute x6, waiting for transfers between devices, local(): lax.ppermute(block, 'inp', [((i + d) % rows, i) for i in range(rows)])  20.9 us
    pallas_call x2, Pallas kernels, correlate(): pl.pallas_call(body, grid=(count,), out_shape=jax.ShapeDtypeStruct(shape,...  12.3 us
    all_to_all x1, waiting for transfers between devices, local(): turned.append(lax.all_to_all(spectrum, TIME, 0, 0, tiled=True))  12.3 us
    ppermute x6, starting transfers between devices, local(): lax.ppermute(block, 'inp', [((i + d) % rows, i) for i in range(rows)])  10.1 us
    ppermute x1, waiting for transfers between devices, local(): right_same = lax.ppermute(same, TIME, route(-1, 0))  9.86 us
    ppermute x1, starting transfers between devices, local(): right_cross = lax.ppermute(cross, TIME, route(-1, 1))  9.16 us
    pallas_call x1, Pallas kernels, filter_bank(): pl.pallas_call(functools.partial(filter_kernel, taps, frames, parts), out...  8.58 us
  transfers between devices with their start and end apart: 12, of which 8 were waited for; matrix products, arithmetic and copies ran while one was open for 1% of the time, Pallas kernels for 4%

profile of v1, /device:TPU:1, one launch (start us, length us, event | category | flops | bytes accessed | tf_op | source)
XLA Modules:
  0.0 134.8 jit_solution(13516207675200623978)
XLA Ops:
  0.0 2.2 %constant_dynamic-slice_fusion = (bf16[4,2,256,128]{3,2,1,0:T(8,128)(2,1)}, bf16[4,2,256,128]{3,2,1,0:T(8,128)(2,1)S(1)}) fusion(bf16[4,2,256,256]{3,2,1,0:T(8,128)(2,1)} %param.6, s32[]{:T(128)S(6)} %select_n.51, s32[]{:T(128)S(6)} %select_n.50), kind=kLoop, calls=%fused_computation.23 | loop fusion | bytes 2097160 | tf_op jit(solution)/shard_map/dynamic_slice | solution.py:172
  2.2 9.2 %collective-permute-start.4 = (bf16[4,2,256,128]{3,2,1,0:T(8,128)(2,1)}, bf16[4,2,256,128]{3,2,1,0:T(8,128)(2,1)S(1)}, u32[]{:S(2)}, u32[]{:S(2)}) collective-permute-start(bf16[4,2,256,128]{3,2,1,0:T(8,128)(2,1)} %get-tuple-element.9), channel_id=1, source_target_pairs={{9,0},{8,1},{17,8},{16,9},{25,16},{24,17},{33,24},{32,25},{41,32},... | collective-permute-start | bytes 1572872 | tf_op jit(solution)/shard_map/halo/ppermute | solution.py:185
  11.3 1.3 collective-permute-start.2
  12.9 4.1 %collective-permute-start.1 = (bf16[4,2,256,128]{3,2,1,0:T(8,128)(2,1)S(1)}, bf16[4,2,256,128]{3,2,1,0:T(8,128)(2,1)}, u32[]{:S(2)}, u32[]{:S(2)}) collective-permute-start(bf16[4,2,256,128]{3,2,1,0:T(8,128)(2,1)S(1)} %get-tuple-element.10.same), channel_id=1, source_target_pairs={{0,8},{1,9},{8,16},{9,17},{16,24},{17,25},{24,32},{25,33},{32,40},... | collective-permute-start | bytes 1572872 | tf_op jit(solution)/shard_map/halo/ppermute | solution.py:188
  17.8 5.6 %collective-permute-done.4.right_cross = bf16[4,2,256,128]{3,2,1,0:T(8,128)(2,1)S(1)} collective-permute-done((bf16[4,2,256,128]{3,2,1,0:T(8,128)(2,1)}, bf16[4,2,256,128]{3,2,1,0:T(8,128)(2,1)S(1)}, u32[]{:S(2)}, u32[]{:S(2)}) %collective-permute-start.4) | collective-permute-done | bytes 524320 | tf_op jit(solution)/shard_map/halo/ppermute | solution.py:185
  23.4 1.3 collective-permute-done.2.left_cross
  24.7 9.9 %collective-permute-done.3.right_same = bf16[4,2,256,128]{3,2,1,0:T(8,128)(2,1)} collective-permute-done((bf16[4,2,256,128]{3,2,1,0:T(8,128)(2,1)S(1)}, bf16[4,2,256,128]{3,2,1,0:T(8,128)(2,1)}, u32[]{:S(2)}, u32[]{:S(2)}) %collective-permute-start.3) | collective-permute-done | bytes 524320 | tf_op jit(solution)/shard_map/halo/ppermute | solution.py:187
  34.5 1.3 collective-permute-done.1.left_same
  35.8 2.6 %broadcast_in_dim.4.coef = f32[16,256,128]{2,1,0:T(8,128)} broadcast(f32[16,256]{1,0:T(8,128)} %param.7), dimensions={0,1} | broadcast | bytes 2113536 | tf_op jit(solution)/shard_map/broadcast_in_dim | solution.py:190
  38.4 8.6 %filter_bank.1 = (bf16[64,32,128]{2,1,0:T(8,128)(2,1)S(1)}, bf16[64,32,128]{2,1,0:T(8,128)(2,1)}) custom-call(s32[2]{0:T(128)S(1)} %pad_add_fusion.place, bf16[4,2,256,128]{3,2,1,0:T(8,128)(2,1)S(1)} %get-tuple-element.10.same, bf16[4,2,256,128]{3,2,1,0:T(8,128)(2,1)S(1)} %collective-permute-done.cross, ...), custom_call_target="tpu_custom_call" | custom-call | tf_op jit(solution)/shard_map/filter/filter_bank/pallas_call | solution.py:105
  47.0 25.4 %all_to_all.10 = bf16[64,32,128]{2,1,0:T(8,128)(2,1)S(1)} all-to-all(bf16[64,32,128]{2,1,0:T(8,128)(2,1)S(1)} %get-tuple-element.8), channel_id=1, replica_groups=mesh['tm'=32,'inp'=4,'integ'=2] {'tm','integ'}, dimensions={0} | all-to-all | bytes 1048576 | tf_op jit(solution)/shard_map/exchange/all_to_all | solution.py:212
  72.4 6.3 %all-to-all-start = ((bf16[64,32,128]{2,1,0:T(8,128)(2,1)}), bf16[64,32,128]{2,1,0:T(8,128)(2,1)S(1)}, u32[]{:S(2)}, u32[]{:S(2)}) async-start(bf16[64,32,128]{2,1,0:T(8,128)(2,1)} %get-tuple-element.7), calls=%async_computation | async-start | bytes 1048576 | tf_op jit(solution)/shard_map/exchange/all_to_all | solution.py:212
  78.7 1.4 %collective-permute-start.10 = (bf16[64,32,128]{2,1,0:T(8,128)(2,1)S(1)}, bf16[64,32,128]{2,1,0:T(8,128)(2,1)S(1)}, u32[]{:S(2)}, u32[]{:S(2)}) collective-permute-start(bf16[64,32,128]{2,1,0:T(8,128)(2,1)S(1)} %all_to_all.10), channel_id=1, source_target_pairs={{6,0},{0,2},{2,4},{4,6},{7,1},{1,3},{3,5},{5,7},{14,8},{8,10},{10,... | collective-permute-start | bytes 1572872 | tf_op jit(solution)/shard_map/gather/ppermute | solution.py:220
  80.0 2.6 %collective-permute-start.9 = (bf16[64,32,128]{2,1,0:T(8,128)(2,1)S(1)}, bf16[64,32,128]{2,1,0:T(8,128)(2,1)S(1)}, u32[]{:S(2)}, u32[]{:S(2)}) collective-permute-start(bf16[64,32,128]{2,1,0:T(8,128)(2,1)S(1)} %all_to_all.10), channel_id=1, source_target_pairs={{4,0},{6,2},{0,4},{2,6},{5,1},{7,3},{1,5},{3,7},{12,8},{14,10},{8,... | collective-permute-start | bytes 1572872 | tf_op jit(solution)/shard_map/gather/ppermute | solution.py:220
  82.7 1.1 collective-permute-start.8
  83.7 12.3 %all-to-all-done = bf16[64,32,128]{2,1,0:T(8,128)(2,1)S(1)} async-done(((bf16[64,32,128]{2,1,0:T(8,128)(2,1)}), bf16[64,32,128]{2,1,0:T(8,128)(2,1)S(1)}, u32[]{:S(2)}, u32[]{:S(2)}) %all-to-all-start) | async-done | bytes 524320 | tf_op jit(solution)/shard_map/exchange/all_to_all | solution.py:212
  96.0 1.3 collective-permute-start.7
  97.3 2.6 %collective-permute-start.6 = (bf16[64,32,128]{2,1,0:T(8,128)(2,1)S(1)}, bf16[64,32,128]{2,1,0:T(8,128)(2,1)}, u32[]{:S(2)}, u32[]{:S(2)}) collective-permute-start(bf16[64,32,128]{2,1,0:T(8,128)(2,1)S(1)} %all-to-all-done), channel_id=1, source_target_pairs={{4,0},{6,2},{0,4},{2,6},{5,1},{7,3},{1,5},{3,7},{12,8},{14,10},{8,... | collective-permute-start | bytes 1572872 | tf_op jit(solution)/shard_map/gather/ppermute | solution.py:220
  99.9 1.1 collective-permute-start.5
  101.6 3.9 %collective-permute-done.9 = bf16[64,32,128]{2,1,0:T(8,128)(2,1)S(1)} collective-permute-done((bf16[64,32,128]{2,1,0:T(8,128)(2,1)S(1)}, bf16[64,32,128]{2,1,0:T(8,128)(2,1)S(1)}, u32[]{:S(2)}, u32[]{:S(2)}) %collective-permute-start.9) | collective-permute-done | bytes 524320 | tf_op jit(solution)/shard_map/gather/ppermute | solution.py:220
  105.5 5.6 %correlate.2.refs_6_ = f32[4,2,256,1024]{3,2,1,0:T(8,128)} custom-call(bf16[32,2,32,128]{3,2,1,0:T(8,128)(2,1)S(1)} %bitcast.12, bf16[32,2,32,128]{3,2,1,0:T(8,128)(2,1)S(1)} %bitcast.16, bf16[32,2,32,128]{3,2,1,0:T(8,128)(2,1)S(1)} %bitcast.15, bf16[32,2,32,128]{3,2,1,0:T(8,128)(2,1)S(1)} %bitcast.14, bf16[1024,1024]{1,0:T(8,128)(2,1)S(1)} %compare_convert_fusion.refs_4_, ...), custom_call_target="tpu_custom_call" | custom-call | tf_op jit(solution)/shard_map/correlate/correlate/pallas_call | solution.py:154
  111.1 7.2 %collective-permute-done.7 = bf16[64,32,128]{2,1,0:T(8,128)(2,1)S(1)} collective-permute-done((bf16[64,32,128]{2,1,0:T(8,128)(2,1)S(1)}, bf16[64,32,128]{2,1,0:T(8,128)(2,1)S(1)}, u32[]{:S(2)}, u32[]{:S(2)}) %collective-permute-start.7) | collective-permute-done | bytes 524320 | tf_op jit(solution)/shard_map/gather/ppermute | solution.py:220
  118.3 9.8 %collective-permute-done.6 = bf16[64,32,128]{2,1,0:T(8,128)(2,1)} collective-permute-done((bf16[64,32,128]{2,1,0:T(8,128)(2,1)S(1)}, bf16[64,32,128]{2,1,0:T(8,128)(2,1)}, u32[]{:S(2)}, u32[]{:S(2)}) %collective-permute-start.6) | collective-permute-done | bytes 524320 | tf_op jit(solution)/shard_map/gather/ppermute | solution.py:220
  128.1 6.8 %correlate.3 = f32[4,2,256,1024]{3,2,1,0:T(8,128)} custom-call(bf16[32,2,32,128]{3,2,1,0:T(8,128)(2,1)S(1)} %bitcast.13, bf16[32,2,32,128]{3,2,1,0:T(8,128)(2,1)} %bitcast.4.refs_1_, bf16[32,2,32,128]{3,2,1,0:T(8,128)(2,1)} %bitcast.5.refs_2_, bf16[32,2,32,128]{3,2,1,0:T(8,128)(2,1)S(1)} %bitcast.17, ...), custom_call_target="tpu_custom_call", output_to_operand_aliasing={{}: (6, {})} | custom-call | tf_op jit(solution)/shard_map/correlate/correlate/pallas_call | solution.py:154
  (19 shorter events, 1.8 us)
Async XLA Ops:
  0.0 38.4 %copy-start = (bf16[512,512]{1,0:T(8,128)(2,1)S(1)}, bf16[512,512]{1,0:T(8,128)(2,1)}, u32[]{:S(2)}) copy-start(bf16[512,512]{1,0:T(8,128)(2,1)} %constant.77.clone.low) | copy-start | bytes 1572868
  0.0 38.4 %copy-start.1 = (bf16[512,512]{1,0:T(8,128)(2,1)S(1)}, bf16[512,512]{1,0:T(8,128)(2,1)}, u32[]{:S(2)}) copy-start(bf16[512,512]{1,0:T(8,128)(2,1)} %constant.76.clone.high) | copy-start | bytes 1572868
  2.2 21.2 %collective-permute-start.4 = (bf16[4,2,256,128]{3,2,1,0:T(8,128)(2,1)}, bf16[4,2,256,128]{3,2,1,0:T(8,128)(2,1)S(1)}, u32[]{:S(2)}, u32[]{:S(2)}) collective-permute-start(bf16[4,2,256,128]{3,2,1,0:T(8,128)(2,1)} %get-tuple-element.9), channel_id=1, source_target_pairs={{9,0},{8,1},{17,8},{16,9},{25,16},{24,17},{33,24},{32,25},{41,32},... | collective-permute-start | bytes 1572872 | tf_op jit(solution)/shard_map/halo/ppermute | solution.py:185
  11.3 13.3 %collective-permute-start.2 = (bf16[4,2,256,128]{3,2,1,0:T(8,128)(2,1)}, bf16[4,2,256,128]{3,2,1,0:T(8,128)(2,1)S(1)}, u32[]{:S(2)}, u32[]{:S(2)}) collective-permute-start(bf16[4,2,256,128]{3,2,1,0:T(8,128)(2,1)} %get-tuple-element.9), channel_id=1, source_target_pairs={{1,8},{0,9},{9,16},{8,17},{17,24},{16,25},{25,32},{24,33},{33,40},... | collective-permute-start | bytes 1572872 | tf_op jit(solution)/shard_map/halo/ppermute | solution.py:186
  12.7 12.0 %collective-permute-start = (bf16[4,2,256,128]{3,2,1,0:T(8,128)(2,1)}, bf16[4,2,256,128]{3,2,1,0:T(8,128)(2,1)S(1)}, u32[]{:S(2)}, u32[]{:S(2)}) collective-permute-start(bf16[4,2,256,128]{3,2,1,0:T(8,128)(2,1)} %get-tuple-element.9), channel_id=1, source_target_pairs={{1,0},{0,1},{9,8},{8,9},{17,16},{16,17},{25,24},{24,25},{33,32},{3... | collective-permute-start | bytes 1572872 | tf_op jit(solution)/shard_map/halo/ppermute | solution.py:189
  12.8 21.8 %collective-permute-start.3 = (bf16[4,2,256,128]{3,2,1,0:T(8,128)(2,1)S(1)}, bf16[4,2,256,128]{3,2,1,0:T(8,128)(2,1)}, u32[]{:S(2)}, u32[]{:S(2)}) collective-permute-start(bf16[4,2,256,128]{3,2,1,0:T(8,128)(2,1)S(1)} %get-tuple-element.10.same), channel_id=1, source_target_pairs={{8,0},{9,1},{16,8},{17,9},{24,16},{25,17},{32,24},{33,25},{40,32},... | collective-permute-start | bytes 1572872 | tf_op jit(solution)/shard_map/halo/ppermute | solution.py:187
  12.9 22.8 %collective-permute-start.1 = (bf16[4,2,256,128]{3,2,1,0:T(8,128)(2,1)S(1)}, bf16[4,2,256,128]{3,2,1,0:T(8,128)(2,1)}, u32[]{:S(2)}, u32[]{:S(2)}) collective-permute-start(bf16[4,2,256,128]{3,2,1,0:T(8,128)(2,1)S(1)} %get-tuple-element.10.same), channel_id=1, source_target_pairs={{0,8},{1,9},{8,16},{9,17},{16,24},{17,25},{24,32},{25,33},{32,40},... | collective-permute-start | bytes 1572872 | tf_op jit(solution)/shard_map/halo/ppermute | solution.py:188
  38.4 62.6 %copy-start.2 = (s32[1024]{0:T(1024)S(1)}, s32[1024]{0:T(1024)}, u32[]{:S(2)}) copy-start(s32[1024]{0:T(1024)} %param.8) | copy-start | bytes 12292
  72.4 23.6 %all-to-all-start = ((bf16[64,32,128]{2,1,0:T(8,128)(2,1)}), bf16[64,32,128]{2,1,0:T(8,128)(2,1)S(1)}, u32[]{:S(2)}, u32[]{:S(2)}) async-start(bf16[64,32,128]{2,1,0:T(8,128)(2,1)} %get-tuple-element.7), calls=%async_computation | async-start | bytes 1048576 | tf_op jit(solution)/shard_map/exchange/all_to_all | solution.py:212
  78.7 21.2 %collective-permute-start.10 = (bf16[64,32,128]{2,1,0:T(8,128)(2,1)S(1)}, bf16[64,32,128]{2,1,0:T(8,128)(2,1)S(1)}, u32[]{:S(2)}, u32[]{:S(2)}) collective-permute-start(bf16[64,32,128]{2,1,0:T(8,128)(2,1)S(1)} %all_to_all.10), channel_id=1, source_target_pairs={{6,0},{0,2},{2,4},{4,6},{7,1},{1,3},{3,5},{5,7},{14,8},{8,10},{10,... | collective-permute-start | bytes 1572872 | tf_op jit(solution)/shard_map/gather/ppermute | solution.py:220
  80.0 25.5 %collective-permute-start.9 = (bf16[64,32,128]{2,1,0:T(8,128)(2,1)S(1)}, bf16[64,32,128]{2,1,0:T(8,128)(2,1)S(1)}, u32[]{:S(2)}, u32[]{:S(2)}) collective-permute-start(bf16[64,32,128]{2,1,0:T(8,128)(2,1)S(1)} %all_to_all.10), channel_id=1, source_target_pairs={{4,0},{6,2},{0,4},{2,6},{5,1},{7,3},{1,5},{3,7},{12,8},{14,10},{8,... | collective-permute-start | bytes 1572872 | tf_op jit(solution)/shard_map/gather/ppermute | solution.py:220
  82.7 22.9 %collective-permute-start.8 = (bf16[64,32,128]{2,1,0:T(8,128)(2,1)S(1)}, bf16[64,32,128]{2,1,0:T(8,128)(2,1)S(1)}, u32[]{:S(2)}, u32[]{:S(2)}) collective-permute-start(bf16[64,32,128]{2,1,0:T(8,128)(2,1)S(1)} %all_to_all.10), channel_id=1, source_target_pairs={{2,0},{4,2},{6,4},{0,6},{3,1},{5,3},{7,5},{1,7},{10,8},{12,10},{14... | collective-permute-start | bytes 1572872 | tf_op jit(solution)/shard_map/gather/ppermute | solution.py:220
  96.0 22.3 %collective-permute-start.7 = (bf16[64,32,128]{2,1,0:T(8,128)(2,1)S(1)}, bf16[64,32,128]{2,1,0:T(8,128)(2,1)S(1)}, u32[]{:S(2)}, u32[]{:S(2)}) collective-permute-start(bf16[64,32,128]{2,1,0:T(8,128)(2,1)S(1)} %all-to-all-done), channel_id=1, source_target_pairs={{6,0},{0,2},{2,4},{4,6},{7,1},{1,3},{3,5},{5,7},{14,8},{8,10},{10,... | collective-permute-start | bytes 1572872 | tf_op jit(solution)/shard_map/gather/ppermute | solution.py:220
  97.3 30.8 %collective-permute-start.6 = (bf16[64,32,128]{2,1,0:T(8,128)(2,1)S(1)}, bf16[64,32,128]{2,1,0:T(8,128)(2,1)}, u32[]{:S(2)}, u32[]{:S(2)}) collective-permute-start(bf16[64,32,128]{2,1,0:T(8,128)(2,1)S(1)} %all-to-all-done), channel_id=1, source_target_pairs={{4,0},{6,2},{0,4},{2,6},{5,1},{7,3},{1,5},{3,7},{12,8},{14,10},{8,... | collective-permute-start | bytes 1572872 | tf_op jit(solution)/shard_map/gather/ppermute | solution.py:220
  99.9 28.2 %collective-permute-start.5 = (bf16[64,32,128]{2,1,0:T(8,128)(2,1)S(1)}, bf16[64,32,128]{2,1,0:T(8,128)(2,1)}, u32[]{:S(2)}, u32[]{:S(2)}) collective-permute-start(bf16[64,32,128]{2,1,0:T(8,128)(2,1)S(1)} %all-to-all-done), channel_id=1, source_target_pairs={{2,0},{4,2},{6,4},{0,6},{3,1},{5,3},{7,5},{1,7},{10,8},{12,10},{14... | collective-permute-start | bytes 1572872 | tf_op jit(solution)/shard_map/gather/ppermute | solution.py:220

commit v2 on v0

v2 whole, which is shorter than its diff:
```python
import functools
import math

import jax
import jax.numpy as jnp
import ml_dtypes
import numpy as np
from jax import lax
from jax.experimental import pallas as pl
from jax.experimental.pallas import tpu as pltpu
from jax.sharding import PartitionSpec as P

TIME = ("tm", "integ")
BF16, F32 = jnp.bfloat16, jnp.float32
LANES = 128
HALF = LANES // 2
BATCHES = 2
VMEM = pl.BlockSpec(memory_space=pltpu.VMEM)
ANY = pl.BlockSpec(memory_space=pl.ANY)
SMEM = pl.BlockSpec(memory_space=pltpu.SMEM)


def fourier_table(channels):
    grid = np.arange(channels)
    angles = (grid[:, None] * grid[None, :] % channels) * (2.0 * math.pi / channels)
    table = np.concatenate([np.cos(angles), np.sin(angles)]) / math.sqrt(channels)
    high = table.astype(ml_dtypes.bfloat16)
    low = (table - high.astype(np.float64)).astype(ml_dtypes.bfloat16)
    return jnp.asarray(high), jnp.asarray(low)


def pack_kernel(voltages, same, cross):
    first = lax.broadcasted_iota(jnp.int32, (voltages.shape[2], LANES), 1) < HALF
    me = lax.axis_index("integ")

    def one_frame(frame, carry):
        for core, out in ((me, same), (1 - me, cross)):
            lanes = pl.ds(pl.multiple_of(core * LANES, LANES), LANES)
            real = voltages[frame, 0, :, lanes].astype(F32)
            imag = voltages[frame, 1, :, lanes].astype(F32)
            out[0, frame] = jnp.where(first, real, pltpu.roll(imag, HALF, 1)).astype(BF16)
            out[1, frame] = jnp.where(first, pltpu.roll(real, HALF, 1), imag).astype(BF16)
        return carry

    lax.fori_loop(0, voltages.shape[0], one_frame, 0)


def pack(voltages):
    frames, _, samples, _ = voltages.shape
    return pl.pallas_call(
        pack_kernel,
        out_shape=[jax.ShapeDtypeStruct((BATCHES, frames, samples, LANES), BF16)] * 2,
        in_specs=[VMEM],
        out_specs=[VMEM] * 2,
        name="pack",
    )(voltages)


def arrange_kernel(same, cross, *outs):
    frames = same.shape[1]
    me = lax.axis_index("integ")
    for batch, out in enumerate(outs):
        out[pl.ds(me * frames, frames)] = same[batch]
        out[pl.ds((1 - me) * frames, frames)] = cross[batch]


def arrange(same, cross):
    batches, frames, samples, _ = same.shape
    return pl.pallas_call(
        arrange_kernel,
        out_shape=[jax.ShapeDtypeStruct((2 * frames, samples, LANES), BF16)] * batches,
        in_specs=[VMEM] * 2,
        out_specs=[VMEM] * batches,
        name="arrange",
    )(same, cross)


def filter_kernel(
    taps, frames, place, left, own, right,
    coef, high, low, valid, out, held, w_high, w_low, turned, sems
):
    wraps = place[0]
    samples = own.shape[1]
    copies = []
    for n, block in enumerate((left, own, right)):
        copies.append(pltpu.make_async_copy(block, held.at[pl.ds(n * frames, frames)], sems.at[n]))
        copies[-1].start()
    for copy in copies:
        copy.wait()

    @pl.when(wraps >= 1)
    def _():
        held[:frames] = jnp.zeros((frames,) + own.shape[1:], BF16)

    @pl.when(wraps == 2)
    def _():
        held[frames : 2 * frames] = jnp.zeros((frames,) + own.shape[1:], BF16)

    rows = 16

    def one_block(block, carry):
        at = pl.ds(pl.multiple_of(block * rows, rows), rows)
        column = coef[at, :]
        factors = [jnp.broadcast_to(column[:, p : p + 1], (rows, LANES)) for p in range(taps)]
        sums = [None] * frames
        for j in range(2 * frames - taps + 1, 3 * frames):
            x = held[j, at, :].astype(F32)
            for o in range(frames):
                p = j - (2 * frames - taps + 1) - o
                if 0 <= p < taps:
                    term = factors[p] * x
                    sums[o] = term if sums[o] is None else sums[o] + term
        for o in range(frames):
            top = sums[o].astype(BF16)
            lanes = slice((o % 2) * LANES, (o % 2 + 1) * LANES)
            w_high[o // 2, at, lanes] = top
            w_low[o // 2, at, lanes] = (sums[o] - top.astype(F32)).astype(BF16)
        return carry

    lax.fori_loop(0, samples // rows, one_block, 0)

    keep = valid[...]
    sign = jnp.where(lax.broadcasted_iota(jnp.int32, (1, LANES), 1) < HALF, 1.0, -1.0).astype(F32)
    for pair in range(frames // 2):
        block = jnp.dot(high[...], w_high[pair], preferred_element_type=F32)
        block += jnp.dot(high[...], w_low[pair], preferred_element_type=F32)
        block += jnp.dot(low[...], w_high[pair], preferred_element_type=F32)
        for which in range(2):
            lanes = slice(which * LANES, (which + 1) * LANES)
            cosines, sines = block[:samples, lanes], block[samples:, lanes]
            spectrum = (cosines + sign * pltpu.roll(sines, HALF, 1)) * keep
            turned[pl.ds(pair * 2 + which, samples, stride=frames), :] = spectrum

    depth = out.shape[1]

    def one_dest(dest, carry):
        out[dest] = turned[pl.ds(pl.multiple_of(dest * depth, depth), depth), :].astype(BF16)
        return carry

    lax.fori_loop(0, out.shape[0], one_dest, 0, unroll=8)


def filter_bank(place, blocks, coef, high, low, valid, dests):
    samples, taps = coef.shape
    frames = blocks[0].shape[0]
    return pl.pallas_call(
        functools.partial(filter_kernel, taps, frames),
        out_shape=jax.ShapeDtypeStruct((dests, samples // dests * frames, LANES), BF16),
        in_specs=[SMEM] + [ANY] * 3 + [VMEM] * 4,
        out_specs=VMEM,
        scratch_shapes=[
            pltpu.VMEM((3 * frames, samples, LANES), BF16),
            pltpu.VMEM((frames // 2, samples, 2 * LANES), BF16),
            pltpu.VMEM((frames // 2, samples, 2 * LANES), BF16),
            pltpu.VMEM((samples * frames, LANES), F32),
            pltpu.SemaphoreType.DMA((3,)),
        ],
        compiler_params=pltpu.CompilerParams(vmem_limit_bytes=12 * 2**20),
        cost_estimate=pl.CostEstimate(flops=20000000000, bytes_accessed=2**20, transcendentals=0),
        name="filter_bank",
    )(place, *blocks, coef, high, low, valid)


def columns_of(pieces):
    first, second = (
        jnp.concatenate([p[:, core].reshape(-1, LANES) for p in pieces], axis=0).astype(F32) for core in range(2)
    )
    lower = lax.broadcasted_iota(jnp.int32, first.shape, 1) < HALF
    real = jnp.where(lower, first, pltpu.roll(second, HALF, 1))
    imag = jnp.where(lower, pltpu.roll(first, HALF, 1), second)
    return jnp.concatenate([real, imag], axis=0).astype(BF16)


def place_inputs(blocks, pick, pick_own, frames, channels):
    gathered = jnp.concatenate([columns_of(b) for b in blocks], axis=1)

    def split(table):
        product = jnp.dot(gathered, table[...], preferred_element_type=F32)
        product = product.reshape(2, -1, channels, frames, table.shape[1])
        return lambda part, channel: product[part, :, channel].reshape(-1, table.shape[1]).astype(BF16)

    every, own = split(pick), split(pick_own)
    result = []
    for channel in range(channels):
        columns = jnp.concatenate([every(0, channel), every(1, channel)], axis=0)
        real, imag = own(0, channel), own(1, channel)
        rows = jnp.concatenate(
            [jnp.concatenate([real, imag], axis=1), jnp.concatenate([imag, -real], axis=1)], axis=0
        )
        result.append((columns, rows))
    return result


def grouped(refs, counts):
    return [refs[sum(counts[:n]) :][:count] for n, count in enumerate(counts)]


def order_kernel(counts, frames, *refs):
    blocks, (pick, pick_own, every, own) = grouped(refs, counts), refs[sum(counts) :]
    for channel, (columns, rows) in enumerate(place_inputs(blocks, pick, pick_own, frames, every.shape[0])):
        every[channel] = columns
        own[channel] = rows


def order_inputs(blocks, picks, frames):
    counts = [len(b) for b in blocks]
    operands = [piece for b in blocks for piece in b] + [*picks]
    channels = blocks[0][0].shape[2] // frames
    depth = 2 * frames * sum(p.shape[0] for p in blocks[0])
    shapes = [(channels, depth, picks[0].shape[1]), (channels, depth, 2 * picks[1].shape[1])]
    flops = 2 * channels * depth * picks[0].shape[0] * (picks[0].shape[1] + picks[1].shape[1])
    return pl.pallas_call(
        functools.partial(order_kernel, counts, frames),
        out_shape=[jax.ShapeDtypeStruct(shape, BF16) for shape in shapes],
        in_specs=[VMEM] * len(operands),
        out_specs=[VMEM] * 2,
        compiler_params=pltpu.CompilerParams(vmem_limit_bytes=30 * 2**20),
        cost_estimate=pl.CostEstimate(flops=flops, bytes_accessed=2**20, transcendentals=0),
        name="order_inputs",
    )(*operands)


def correlate_kernel(scale, counts, frames, *refs):
    blocks, (pick, pick_own, early, early_own, out, every, own) = grouped(refs, counts), refs[sum(counts) :]
    channel = pl.program_id(0)
    width = out.shape[2]

    @pl.when(channel == 0)
    def _():
        for n, (columns, rows) in enumerate(place_inputs(blocks, pick, pick_own, frames, every.shape[0])):
            every[n] = columns + early[n]
            own[n] = rows + early_own[n]

    product = lax.dot_general(
        own[channel], every[channel], (((0,), (0,)), ((), ())), preferred_element_type=F32
    )
    out[0, 0] = product[:width] * scale
    out[0, 1] = product[width:] * scale


def correlate(blocks, picks, early, scale, frames, shape):
    counts = [len(b) for b in blocks]
    operands = [piece for b in blocks for piece in b] + [*picks, *early]
    return pl.pallas_call(
        functools.partial(correlate_kernel, scale, counts, frames),
        grid=(shape[0],),
        out_shape=jax.ShapeDtypeStruct(shape, F32),
        in_specs=[VMEM] * len(operands),
        out_specs=pl.BlockSpec((1,) + shape[1:], lambda i: (i, 0, 0, 0)),
        scratch_shapes=[pltpu.VMEM(a.shape, BF16) for a in early],
        compiler_params=pltpu.CompilerParams(vmem_limit_bytes=32 * 2**20),
        name="correlate",
    )(*operands)


def local(voltages, taps_coef, station_map, flags):
    frames, _, samples, width = voltages.shape
    chips, cores, rows = lax.axis_size("tm"), lax.axis_size("integ"), lax.axis_size("inp")
    chip, core, row = lax.axis_index("tm"), lax.axis_index("integ"), lax.axis_index("inp")
    index = lambda t, c: t * cores + c
    dests, chip_frames, inputs = chips * cores, frames * cores, width * rows
    wraps = jnp.where(chip == chips - 1, 2, jnp.where(chip == 0, 1, 0))
    place = wraps.astype(jnp.int32)[None]

    def route(step, swap):
        return [(index((t - step) % chips, c ^ swap), index(t, c)) for t in range(chips) for c in range(cores)]

    with jax.named_scope("halo"):
        same, cross = pack(voltages)
        owns = arrange(same, lax.ppermute(cross, TIME, route(0, 1)))
        halos = [(lax.ppermute(o, TIME, route(1, 0)), o, lax.ppermute(o, TIME, route(-1, 0))) for o in owns]

    coef = taps_coef.T
    high, low = fourier_table(samples)
    valid = (1 - flags).astype(F32)

    own_slots = lax.dynamic_slice_in_dim(station_map, row * width, width)

    def picks(blocks):
        at = jnp.arange(LANES, dtype=jnp.int32)
        held = [(row + turn) % rows * width + at // HALF * LANES + batch * HALF + at % HALF for turn, batch in blocks]
        held = jnp.concatenate(held)
        return [(held[:, None] == slots[None, :]).astype(BF16) for slots in (station_map, own_slots)]

    up = [((i + 1) % rows, i) for i in range(rows)]
    down = [((i - 1) % rows, i) for i in range(rows)]
    shape = (samples // dests, 2, width, inputs)
    scale = 1.0 / (frames * dests)
    near, far = [], []
    for batch in range(BATCHES):
        flagged = lax.dynamic_slice_in_dim(valid, core * LANES + batch * HALF, HALF)
        keep = jnp.concatenate([flagged, flagged])[None, :]
        with jax.named_scope("filter"):
            spectra = filter_bank(place, halos[batch], coef, high, low, keep, dests)
        with jax.named_scope("exchange"):
            block = lax.all_to_all(spectra, TIME, 0, 0, tiled=True)
        block = block.reshape(chips, cores, -1, LANES)
        with jax.named_scope("gather"):
            above, below = lax.ppermute(block, "inp", up), lax.ppermute(block, "inp", down)
            half = chips // 2
            far.append([lax.ppermute(above[:half], "inp", up), lax.ppermute(below[half:], "inp", down)])
        near += [[block], [above], [below]]
    with jax.named_scope("order"):
        table = picks([(turn, batch) for batch in range(BATCHES) for turn in (0, 1, 3)])
        early = order_inputs(near, table, chip_frames)
    with jax.named_scope("correlate"):
        out = correlate(far, picks([(2, batch) for batch in range(BATCHES)]), early, scale, chip_frames, shape)
    return out


def solution(mesh):
    return jax.shard_map(
        local,
        mesh=mesh,
        in_specs=(P(("tm", "integ"), None, None, "inp"), P(), P(), P("inp")),
        out_specs=P(("tm", "integ"), None, "inp", None),
        check_vma=False,
    )
```

time: 279 us -> 121 us (0.43)
  waiting for transfers between devices: 146 us -> 50.2 us
  blocking collectives: 40.3 us -> 0 us
  local copies, waits for them, and re-layouts: 37.8 us -> 4.81 us
  Pallas kernels: 0 us -> 25.6 us
  starting transfers between devices: 17.4 us -> 38.4 us
  between operations: 13.7 us -> 0.28 us
  matrix products: 12.5 us -> 0 us
  other arithmetic: 11 us -> 1.66 us
    ppermute x4 -> x13, waiting for transfers between devices: 99.1 us -> 23.5 us  [the longest x2 8.31 us: local(): lax.ppermute(block, 'inp', down)]
    all_gather x1 -> x0, waiting for transfers between devices: 46.5 us -> none  [local(): gathered = lax.all_gather(turned, 'inp', axis=3, tiled=True)]
    all_to_all x1 -> x0, blocking collectives: 40.3 us -> none  [local(): lax.all_to_all(channel_spectra, ('tm', 'integ'), split_axis=2, concat_axi...]
    all_to_all x0 -> x2, waiting for transfers between devices: none -> 26.7 us  [local(): block = lax.all_to_all(spectra, TIME, 0, 0, tiled=True)]
    pallas_call x0 -> x6, Pallas kernels: none -> 25.6 us  [the longest x2 9.24 us: filter_bank(): pl.pallas_call(functools.partial(filter_kernel, taps, frames), out_shape=...]
    gather x3 -> x0, local copies, waits for them, and re-layouts: 18.3 us -> none  [the longest x1 13.2 us: local(): col_block = jnp.take(gathered, station_map, axis=3)]
    all_to_all x0 -> x2, starting transfers between devices: none -> 13.1 us  [local(): block = lax.all_to_all(spectra, TIME, 0, 0, tiled=True)]
    dot_general x3 -> x0, matrix products: 12.5 us -> none  [the longest x1 9.91 us: local(): jnp.einsum('oicn,fina->foca', dft_table, windowed, precision=lax.Precisio...]
  transfers between devices with their start and end apart: 5 -> 15, of which waited for: 4 -> 7; matrix products, arithmetic and copies ran while one was open for 1% -> 2% of each run, Pallas kernels for 0% -> 12%
where the time goes in v2:
time: 121 us
  waiting for transfers between devices  50.2 us (41%)
  starting transfers between devices  38.4 us (32%)
  Pallas kernels  25.6 us (21%)
  local copies, waits for them, and re-layouts  4.81 us (4%)
  other arithmetic  1.66 us (1%)
    all_to_all x2, waiting for transfers between devices, local(): block = lax.all_to_all(spectra, TIME, 0, 0, tiled=True)  26.7 us
    all_to_all x2, starting transfers between devices, local(): block = lax.all_to_all(spectra, TIME, 0, 0, tiled=True)  13.1 us
    ppermute x2, starting transfers between devices, local(): lax.ppermute(o, TIME, route(-1, 0))  10.8 us
    pallas_call x2, Pallas kernels, filter_bank(): pl.pallas_call(functools.partial(filter_kernel, taps, frames), out_shape=...  9.24 us
    ppermute x2, waiting for transfers between devices, local(): lax.ppermute(block, 'inp', down)  8.31 us
    pallas_call x1, Pallas kernels, correlate(): pl.pallas_call(functools.partial(correlate_kernel, scale, counts, frames)...  6.63 us
    ppermute x2, waiting for transfers between devices, local(): lax.ppermute(o, TIME, route(-1, 0))  5.55 us
    ppermute x2, starting transfers between devices, local(): lax.ppermute(above[:half], 'inp', up)  5.46 us
  transfers between devices with their start and end apart: 15, of which 7 were waited for; matrix products, arithmetic and copies ran while one was open for 2% of the time, Pallas kernels for 12%

profile of v2, /device:TPU:1, one launch (start us, length us, event | category | flops | bytes accessed | tf_op | source)
XLA Modules:
  0.0 121.0 jit_solution(12140460738154311363)
XLA Ops:
  0.0 2.7 %pack.1 = (bf16[2,4,256,128]{3,2,1,0:T(8,128)(2,1)}, bf16[2,4,256,128]{3,2,1,0:T(8,128)(2,1)}) custom-call(bf16[4,2,256,256]{3,2,1,0:T(8,128)(2,1)} %voltages.1), custom_call_target="tpu_custom_call" | custom-call | tf_op jit(solution)/shard_map/halo/pack/pallas_call | solution.py:50
  2.7 3.2 %collective-permute-start = (bf16[2,4,256,128]{3,2,1,0:T(8,128)(2,1)}, bf16[2,4,256,128]{3,2,1,0:T(8,128)(2,1)S(1)}, u32[]{:S(2)}, u32[]{:S(2)}) collective-permute-start(bf16[2,4,256,128]{3,2,1,0:T(8,128)(2,1)} %get-tuple-element.12), channel_id=1, source_target_pairs={{1,0},{0,1},{9,8},{8,9},{17,16},{16,17},{25,24},{24,25},{33,32},{3... | collective-permute-start | bytes 1572872 | tf_op jit(solution)/shard_map/halo/ppermute | solution.py:270
  8.5 2.3 %arrange.1 = (bf16[8,256,128]{2,1,0:T(8,128)(2,1)}, bf16[8,256,128]{2,1,0:T(8,128)(2,1)}) custom-call(bf16[2,4,256,128]{3,2,1,0:T(8,128)(2,1)} %get-tuple-element.11.same, bf16[2,4,256,128]{3,2,1,0:T(8,128)(2,1)} %copy-done.6), custom_call_target="tpu_custom_call" | custom-call | tf_op jit(solution)/shard_map/halo/arrange/pallas_call | solution.py:69
  10.8 6.0 %collective-permute-start.2 = (bf16[8,256,128]{2,1,0:T(8,128)(2,1)}, bf16[8,256,128]{2,1,0:T(8,128)(2,1)S(1)}, u32[]{:S(2)}, u32[]{:S(2)}) collective-permute-start(bf16[8,256,128]{2,1,0:T(8,128)(2,1)} %get-tuple-element.13.own), channel_id=1, source_target_pairs={{8,0},{9,1},{16,8},{17,9},{24,16},{25,17},{32,24},{33,25},{40,32},... | collective-permute-start | bytes 1572872 | tf_op jit(solution)/shard_map/halo/ppermute | solution.py:271
  17.8 4.8 %collective-permute-start.8 = (bf16[8,256,128]{2,1,0:T(8,128)(2,1)}, bf16[8,256,128]{2,1,0:T(8,128)(2,1)S(1)}, u32[]{:S(2)}, u32[]{:S(2)}) collective-permute-start(bf16[8,256,128]{2,1,0:T(8,128)(2,1)} %get-tuple-element.14.own), channel_id=1, source_target_pairs={{8,0},{9,1},{16,8},{17,9},{24,16},{25,17},{32,24},{33,25},{40,32},... | collective-permute-start | bytes 1572872 | tf_op jit(solution)/shard_map/halo/ppermute | solution.py:271
  22.6 5.5 %collective-permute-done.2.right = bf16[8,256,128]{2,1,0:T(8,128)(2,1)S(1)} collective-permute-done((bf16[8,256,128]{2,1,0:T(8,128)(2,1)}, bf16[8,256,128]{2,1,0:T(8,128)(2,1)S(1)}, u32[]{:S(2)}, u32[]{:S(2)}) %collective-permute-start.2) | collective-permute-done | bytes 524320 | tf_op jit(solution)/shard_map/halo/ppermute | solution.py:271
  28.1 5.1 %collective-permute-done.1.left = bf16[8,256,128]{2,1,0:T(8,128)(2,1)S(1)} collective-permute-done((bf16[8,256,128]{2,1,0:T(8,128)(2,1)}, bf16[8,256,128]{2,1,0:T(8,128)(2,1)S(1)}, u32[]{:S(2)}, u32[]{:S(2)}) %collective-permute-start.1) | collective-permute-done | bytes 524320 | tf_op jit(solution)/shard_map/halo/ppermute | solution.py:271
  33.2 1.0 copy-done.1
  36.1 4.6 %filter_bank.2 = bf16[64,32,128]{2,1,0:T(8,128)(2,1)} custom-call(s32[1]{0:T(128)} %bitcast.place, bf16[8,256,128]{2,1,0:T(8,128)(2,1)S(1)} %collective-permute-done.1.left, bf16[8,256,128]{2,1,0:T(8,128)(2,1)S(1)} %copy-done.1, bf16[8,256,128]{2,1,0:T(8,128)(2,1)S(1)} %collective-permute-done.2.right, f32[256,16]{1,0:T(8,128)S(1)} %bitcast.14, ...), custom_call_target="tpu_custom_call" | custom-call | flops 20000000000 | bytes 1048576 | tf_op jit(solution)/shard_map/filter/filter_bank/pallas_call | solution.py:146
  40.8 6.7 %all-to-all-start = ((bf16[64,32,128]{2,1,0:T(8,128)(2,1)}), bf16[64,32,128]{2,1,0:T(8,128)(2,1)S(1)}, u32[]{:S(2)}, u32[]{:S(2)}) async-start(bf16[64,32,128]{2,1,0:T(8,128)(2,1)} %filter_bank.2), calls=%async_computation | async-start | bytes 1048576 | tf_op jit(solution)/shard_map/exchange/all_to_all | solution.py:296
  47.6 4.6 %filter_bank.3 = bf16[64,32,128]{2,1,0:T(8,128)(2,1)} custom-call(s32[1]{0:T(128)} %bitcast.place, bf16[8,256,128]{2,1,0:T(8,128)(2,1)S(1)} %collective-permute-done.7.left, bf16[8,256,128]{2,1,0:T(8,128)(2,1)S(1)} %copy-done, bf16[8,256,128]{2,1,0:T(8,128)(2,1)S(1)} %collective-permute-done.8.right, f32[256,16]{1,0:T(8,128)S(1)} %bitcast.15, ...), custom_call_target="tpu_custom_call" | custom-call | flops 20000000000 | bytes 1048576 | tf_op jit(solution)/shard_map/filter/filter_bank/pallas_call | solution.py:146
  52.2 12.7 %all-to-all-done = bf16[64,32,128]{2,1,0:T(8,128)(2,1)S(1)} async-done(((bf16[64,32,128]{2,1,0:T(8,128)(2,1)}), bf16[64,32,128]{2,1,0:T(8,128)(2,1)S(1)}, u32[]{:S(2)}, u32[]{:S(2)}) %all-to-all-start) | async-done | bytes 524320 | tf_op jit(solution)/shard_map/exchange/all_to_all | solution.py:296
  64.9 6.4 %all-to-all-start.1 = ((bf16[64,32,128]{2,1,0:T(8,128)(2,1)}), bf16[64,32,128]{2,1,0:T(8,128)(2,1)S(1)}, u32[]{:S(2)}, u32[]{:S(2)}) async-start(bf16[64,32,128]{2,1,0:T(8,128)(2,1)} %filter_bank.3), calls=%async_computation.1 | async-start | bytes 1048576 | tf_op jit(solution)/shard_map/exchange/all_to_all | solution.py:296
  71.6 1.4 %collective-permute-start.5 = (bf16[32,2,32,128]{3,2,1,0:T(8,128)(2,1)S(1)}, bf16[32,2,32,128]{3,2,1,0:T(8,128)(2,1)S(1)}, u32[]{:S(2)}, u32[]{:S(2)}) collective-permute-start(bf16[32,2,32,128]{3,2,1,0:T(8,128)(2,1)S(1)} %bitcast.8), channel_id=1, source_target_pairs={{6,0},{0,2},{2,4},{4,6},{7,1},{1,3},{3,5},{5,7},{14,8},{8,10},{10,... | collective-permute-start | bytes 1572872 | tf_op jit(solution)/shard_map/gather/ppermute | solution.py:299
  73.0 1.5 %collective-permute-start.3 = (bf16[32,2,32,128]{3,2,1,0:T(8,128)(2,1)S(1)}, bf16[32,2,32,128]{3,2,1,0:T(8,128)(2,1)S(1)}, u32[]{:S(2)}, u32[]{:S(2)}) collective-permute-start(bf16[32,2,32,128]{3,2,1,0:T(8,128)(2,1)S(1)} %bitcast.9), channel_id=1, source_target_pairs={{2,0},{4,2},{6,4},{0,6},{3,1},{5,3},{7,5},{1,7},{10,8},{12,10},{14... | collective-permute-start | bytes 1572872 | tf_op jit(solution)/shard_map/gather/ppermute | solution.py:299
  74.5 14.0 %all-to-all-done.1 = bf16[64,32,128]{2,1,0:T(8,128)(2,1)S(1)} async-done(((bf16[64,32,128]{2,1,0:T(8,128)(2,1)}), bf16[64,32,128]{2,1,0:T(8,128)(2,1)S(1)}, u32[]{:S(2)}, u32[]{:S(2)}) %all-to-all-start.1) | async-done | bytes 524320 | tf_op jit(solution)/shard_map/exchange/all_to_all | solution.py:296
  88.6 1.3 %collective-permute-start.11 = (bf16[32,2,32,128]{3,2,1,0:T(8,128)(2,1)S(1)}, bf16[32,2,32,128]{3,2,1,0:T(8,128)(2,1)S(1)}, u32[]{:S(2)}, u32[]{:S(2)}) collective-permute-start(bf16[32,2,32,128]{3,2,1,0:T(8,128)(2,1)S(1)} %bitcast.11), channel_id=1, source_target_pairs={{6,0},{0,2},{2,4},{4,6},{7,1},{1,3},{3,5},{5,7},{14,8},{8,10},{10,... | collective-permute-start | bytes 1572872 | tf_op jit(solution)/shard_map/gather/ppermute | solution.py:299
  89.8 1.4 %collective-permute-start.9 = (bf16[32,2,32,128]{3,2,1,0:T(8,128)(2,1)S(1)}, bf16[32,2,32,128]{3,2,1,0:T(8,128)(2,1)S(1)}, u32[]{:S(2)}, u32[]{:S(2)}) collective-permute-start(bf16[32,2,32,128]{3,2,1,0:T(8,128)(2,1)S(1)} %bitcast.12), channel_id=1, source_target_pairs={{2,0},{4,2},{6,4},{0,6},{3,1},{5,3},{7,5},{1,7},{10,8},{12,10},{14... | collective-permute-start | bytes 1572872 | tf_op jit(solution)/shard_map/gather/ppermute | solution.py:299
  92.1 2.7 %collective-permute-start.4 = (bf16[16,2,32,128]{3,2,1,0:T(8,128)(2,1)S(1)}, bf16[16,2,32,128]{3,2,1,0:T(8,128)(2,1)S(1)}, u32[]{:S(2)}, u32[]{:S(2)}) collective-permute-start(bf16[16,2,32,128]{3,2,1,0:T(8,128)(2,1)S(1)} %slice.16), channel_id=1, source_target_pairs={{2,0},{4,2},{6,4},{0,6},{3,1},{5,3},{7,5},{1,7},{10,8},{12,10},{14... | collective-permute-start | bytes 786440 | tf_op jit(solution)/shard_map/gather/ppermute | solution.py:301
  94.8 8.3 %collective-permute-done.11.refs_5_ = bf16[32,2,32,128]{3,2,1,0:T(8,128)(2,1)S(1)} collective-permute-done((bf16[32,2,32,128]{3,2,1,0:T(8,128)(2,1)S(1)}, bf16[32,2,32,128]{3,2,1,0:T(8,128)(2,1)S(1)}, u32[]{:S(2)}, u32[]{:S(2)}) %collective-permute-start.11) | collective-permute-done | bytes 524320 | tf_op jit(solution)/shard_map/gather/ppermute | solution.py:299
  103.2 2.7 %collective-permute-start.10 = (bf16[16,2,32,128]{3,2,1,0:T(8,128)(2,1)S(1)}, bf16[16,2,32,128]{3,2,1,0:T(8,128)(2,1)S(1)}, u32[]{:S(2)}, u32[]{:S(2)}) collective-permute-start(bf16[16,2,32,128]{3,2,1,0:T(8,128)(2,1)S(1)} %slice.18), channel_id=1, source_target_pairs={{2,0},{4,2},{6,4},{0,6},{3,1},{5,3},{7,5},{1,7},{10,8},{12,10},{14... | collective-permute-start | bytes 786440 | tf_op jit(solution)/shard_map/gather/ppermute | solution.py:301
  106.0 4.7 %order_inputs.1 = (bf16[4,512,1024]{2,1,0:T(8,128)(2,1)S(1)}, bf16[4,512,512]{2,1,0:T(8,128)(2,1)S(1)}) custom-call(bf16[32,2,32,128]{3,2,1,0:T(8,128)(2,1)S(1)} %bitcast.10, bf16[32,2,32,128]{3,2,1,0:T(8,128)(2,1)S(1)} %collective-permute-done.3.refs_1_, bf16[32,2,32,128]{3,2,1,0:T(8,128)(2,1)S(1)} %collective-permute-done.5.refs_2_, ...), custom_call_target="tpu_custom_call" | custom-call | flops 4026531840 | bytes 1048576 | tf_op jit(solution)/shard_map/order/order_inputs/pallas_call | solution.py:212
  110.7 3.6 %collective-permute-done.12.refs_3_ = bf16[16,2,32,128]{3,2,1,0:T(8,128)(2,1)S(1)} collective-permute-done((bf16[16,2,32,128]{3,2,1,0:T(8,128)(2,1)S(1)}, bf16[16,2,32,128]{3,2,1,0:T(8,128)(2,1)S(1)}, u32[]{:S(2)}, u32[]{:S(2)}) %collective-permute-start.12) | collective-permute-done | bytes 262176 | tf_op jit(solution)/shard_map/gather/ppermute | solution.py:301
  114.3 6.6 %correlate.1 = f32[4,2,256,1024]{3,2,1,0:T(8,128)} custom-call(bf16[16,2,32,128]{3,2,1,0:T(8,128)(2,1)S(1)} %collective-permute-done.4.refs_0_, bf16[16,2,32,128]{3,2,1,0:T(8,128)(2,1)S(1)} %collective-permute-done.6.refs_1_, bf16[16,2,32,128]{3,2,1,0:T(8,128)(2,1)S(1)} %collective-permute-done.10.refs_2_, ...), custom_call_target="tpu_custom_call" | custom-call | tf_op jit(solution)/shard_map/correlate/correlate/pallas_call | solution.py:244
  (51 shorter events, 6.6 us)
Async XLA Ops:
  2.7 5.0 %collective-permute-start = (bf16[2,4,256,128]{3,2,1,0:T(8,128)(2,1)}, bf16[2,4,256,128]{3,2,1,0:T(8,128)(2,1)S(1)}, u32[]{:S(2)}, u32[]{:S(2)}) collective-permute-start(bf16[2,4,256,128]{3,2,1,0:T(8,128)(2,1)} %get-tuple-element.12), channel_id=1, source_target_pairs={{1,0},{0,1},{9,8},{8,9},{17,16},{16,17},{25,24},{24,25},{33,32},{3... | collective-permute-start | bytes 1572872 | tf_op jit(solution)/shard_map/halo/ppermute | solution.py:270
  7.7 0.8 copy-start.6
  10.8 17.3 %collective-permute-start.2 = (bf16[8,256,128]{2,1,0:T(8,128)(2,1)}, bf16[8,256,128]{2,1,0:T(8,128)(2,1)S(1)}, u32[]{:S(2)}, u32[]{:S(2)}) collective-permute-start(bf16[8,256,128]{2,1,0:T(8,128)(2,1)} %get-tuple-element.13.own), channel_id=1, source_target_pairs={{8,0},{9,1},{16,8},{17,9},{24,16},{25,17},{32,24},{33,25},{40,32},... | collective-permute-start | bytes 1572872 | tf_op jit(solution)/shard_map/halo/ppermute | solution.py:271
  16.8 16.3 %collective-permute-start.1 = (bf16[8,256,128]{2,1,0:T(8,128)(2,1)}, bf16[8,256,128]{2,1,0:T(8,128)(2,1)S(1)}, u32[]{:S(2)}, u32[]{:S(2)}) collective-permute-start(bf16[8,256,128]{2,1,0:T(8,128)(2,1)} %get-tuple-element.13.own), channel_id=1, source_target_pairs={{248,0},{249,1},{0,8},{1,9},{8,16},{9,17},{16,24},{17,25},{24,32},... | collective-permute-start | bytes 1572872 | tf_op jit(solution)/shard_map/halo/ppermute | solution.py:271
  17.8 29.8 %collective-permute-start.8 = (bf16[8,256,128]{2,1,0:T(8,128)(2,1)}, bf16[8,256,128]{2,1,0:T(8,128)(2,1)S(1)}, u32[]{:S(2)}, u32[]{:S(2)}) collective-permute-start(bf16[8,256,128]{2,1,0:T(8,128)(2,1)} %get-tuple-element.14.own), channel_id=1, source_target_pairs={{8,0},{9,1},{16,8},{17,9},{24,16},{25,17},{32,24},{33,25},{40,32},... | collective-permute-start | bytes 1572872 | tf_op jit(solution)/shard_map/halo/ppermute | solution.py:271
  22.6 25.0 %collective-permute-start.7 = (bf16[8,256,128]{2,1,0:T(8,128)(2,1)}, bf16[8,256,128]{2,1,0:T(8,128)(2,1)S(1)}, u32[]{:S(2)}, u32[]{:S(2)}) collective-permute-start(bf16[8,256,128]{2,1,0:T(8,128)(2,1)} %get-tuple-element.14.own), channel_id=1, source_target_pairs={{248,0},{249,1},{0,8},{1,9},{8,16},{9,17},{16,24},{17,25},{24,32},... | collective-permute-start | bytes 1572872 | tf_op jit(solution)/shard_map/halo/ppermute | solution.py:271
  33.2 1.0 copy-start.1
  34.2 0.9 copy-start.2
  35.2 0.9 copy-start.4
  36.1 11.4 %copy-start = (bf16[8,256,128]{2,1,0:T(8,128)(2,1)S(1)}, bf16[8,256,128]{2,1,0:T(8,128)(2,1)}, u32[]{:S(2)}) copy-start(bf16[8,256,128]{2,1,0:T(8,128)(2,1)} %get-tuple-element.14.own) | copy-start | bytes 1572868
  36.1 11.4 %copy-start.3 = (bf16[512,256]{1,0:T(8,128)(2,1)S(1)}, bf16[512,256]{1,0:T(8,128)(2,1)}, u32[]{:S(2)}) copy-start(bf16[512,256]{1,0:T(8,128)(2,1)} %constant.134.clone.low) | copy-start | bytes 786436
  36.1 11.4 %copy-start.5 = (bf16[512,256]{1,0:T(8,128)(2,1)S(1)}, bf16[512,256]{1,0:T(8,128)(2,1)}, u32[]{:S(2)}) copy-start(bf16[512,256]{1,0:T(8,128)(2,1)} %constant.133.clone.high) | copy-start | bytes 786436
  40.8 24.1 %all-to-all-start = ((bf16[64,32,128]{2,1,0:T(8,128)(2,1)}), bf16[64,32,128]{2,1,0:T(8,128)(2,1)S(1)}, u32[]{:S(2)}, u32[]{:S(2)}) async-start(bf16[64,32,128]{2,1,0:T(8,128)(2,1)} %filter_bank.2), calls=%async_computation | async-start | bytes 1048576 | tf_op jit(solution)/shard_map/exchange/all_to_all | solution.py:296
  47.5 23.8 %copy-start.7 = (s32[1024]{0:T(1024)S(1)}, s32[1024]{0:T(1024)}, u32[]{:S(2)}) copy-start(s32[1024]{0:T(1024)} %param.8) | copy-start | bytes 12292
  64.9 23.7 %all-to-all-start.1 = ((bf16[64,32,128]{2,1,0:T(8,128)(2,1)}), bf16[64,32,128]{2,1,0:T(8,128)(2,1)S(1)}, u32[]{:S(2)}, u32[]{:S(2)}) async-start(bf16[64,32,128]{2,1,0:T(8,128)(2,1)} %filter_bank.3), calls=%async_computation.1 | async-start | bytes 1048576 | tf_op jit(solution)/shard_map/exchange/all_to_all | solution.py:296
  71.6 20.2 %collective-permute-start.5 = (bf16[32,2,32,128]{3,2,1,0:T(8,128)(2,1)S(1)}, bf16[32,2,32,128]{3,2,1,0:T(8,128)(2,1)S(1)}, u32[]{:S(2)}, u32[]{:S(2)}) collective-permute-start(bf16[32,2,32,128]{3,2,1,0:T(8,128)(2,1)S(1)} %bitcast.8), channel_id=1, source_target_pairs={{6,0},{0,2},{2,4},{4,6},{7,1},{1,3},{3,5},{5,7},{14,8},{8,10},{10,... | collective-permute-start | bytes 1572872 | tf_op jit(solution)/shard_map/gather/ppermute | solution.py:299
  73.0 19.0 %collective-permute-start.3 = (bf16[32,2,32,128]{3,2,1,0:T(8,128)(2,1)S(1)}, bf16[32,2,32,128]{3,2,1,0:T(8,128)(2,1)S(1)}, u32[]{:S(2)}, u32[]{:S(2)}) collective-permute-start(bf16[32,2,32,128]{3,2,1,0:T(8,128)(2,1)S(1)} %bitcast.9), channel_id=1, source_target_pairs={{2,0},{4,2},{6,4},{0,6},{3,1},{5,3},{7,5},{1,7},{10,8},{12,10},{14... | collective-permute-start | bytes 1572872 | tf_op jit(solution)/shard_map/gather/ppermute | solution.py:299
  88.6 14.5 %collective-permute-start.11 = (bf16[32,2,32,128]{3,2,1,0:T(8,128)(2,1)S(1)}, bf16[32,2,32,128]{3,2,1,0:T(8,128)(2,1)S(1)}, u32[]{:S(2)}, u32[]{:S(2)}) collective-permute-start(bf16[32,2,32,128]{3,2,1,0:T(8,128)(2,1)S(1)} %bitcast.11), channel_id=1, source_target_pairs={{6,0},{0,2},{2,4},{4,6},{7,1},{1,3},{3,5},{5,7},{14,8},{8,10},{10,... | collective-permute-start | bytes 1572872 | tf_op jit(solution)/shard_map/gather/ppermute | solution.py:299
  89.8 13.4 %collective-permute-start.9 = (bf16[32,2,32,128]{3,2,1,0:T(8,128)(2,1)S(1)}, bf16[32,2,32,128]{3,2,1,0:T(8,128)(2,1)S(1)}, u32[]{:S(2)}, u32[]{:S(2)}) collective-permute-start(bf16[32,2,32,128]{3,2,1,0:T(8,128)(2,1)S(1)} %bitcast.12), channel_id=1, source_target_pairs={{2,0},{4,2},{6,4},{0,6},{3,1},{5,3},{7,5},{1,7},{10,8},{12,10},{14... | collective-permute-start | bytes 1572872 | tf_op jit(solution)/shard_map/gather/ppermute | solution.py:299
  91.9 18.8 %collective-permute-start.6 = (bf16[16,2,32,128]{3,2,1,0:T(8,128)(2,1)S(1)}, bf16[16,2,32,128]{3,2,1,0:T(8,128)(2,1)S(1)}, u32[]{:S(2)}, u32[]{:S(2)}) collective-permute-start(bf16[16,2,32,128]{3,2,1,0:T(8,128)(2,1)S(1)} %slice.17), channel_id=1, source_target_pairs={{6,0},{0,2},{2,4},{4,6},{7,1},{1,3},{3,5},{5,7},{14,8},{8,10},{10,... | collective-permute-start | bytes 786440 | tf_op jit(solution)/shard_map/gather/ppermute | solution.py:301
  92.1 18.6 %collective-permute-start.4 = (bf16[16,2,32,128]{3,2,1,0:T(8,128)(2,1)S(1)}, bf16[16,2,32,128]{3,2,1,0:T(8,128)(2,1)S(1)}, u32[]{:S(2)}, u32[]{:S(2)}) collective-permute-start(bf16[16,2,32,128]{3,2,1,0:T(8,128)(2,1)S(1)} %slice.16), channel_id=1, source_target_pairs={{2,0},{4,2},{6,4},{0,6},{3,1},{5,3},{7,5},{1,7},{10,8},{12,10},{14... | collective-permute-start | bytes 786440 | tf_op jit(solution)/shard_map/gather/ppermute | solution.py:301
  103.1 11.2 %collective-permute-start.12 = (bf16[16,2,32,128]{3,2,1,0:T(8,128)(2,1)S(1)}, bf16[16,2,32,128]{3,2,1,0:T(8,128)(2,1)S(1)}, u32[]{:S(2)}, u32[]{:S(2)}) collective-permute-start(bf16[16,2,32,128]{3,2,1,0:T(8,128)(2,1)S(1)} %slice.19), channel_id=1, source_target_pairs={{6,0},{0,2},{2,4},{4,6},{7,1},{1,3},{3,5},{5,7},{14,8},{8,10},{10,... | collective-permute-start | bytes 786440 | tf_op jit(solution)/shard_map/gather/ppermute | solution.py:301
  103.2 11.1 %collective-permute-start.10 = (bf16[16,2,32,128]{3,2,1,0:T(8,128)(2,1)S(1)}, bf16[16,2,32,128]{3,2,1,0:T(8,128)(2,1)S(1)}, u32[]{:S(2)}, u32[]{:S(2)}) collective-permute-start(bf16[16,2,32,128]{3,2,1,0:T(8,128)(2,1)S(1)} %slice.18), channel_id=1, source_target_pairs={{2,0},{4,2},{6,4},{0,6},{3,1},{5,3},{7,5},{1,7},{10,8},{12,10},{14... | collective-permute-start | bytes 786440 | tf_op jit(solution)/shard_map/gather/ppermute | solution.py:301

commit v3 on v2

--- a/solution.py
+++ b/solution.py
@@ -26,7 +26,22 @@
     table = np.concatenate([np.cos(angles), np.sin(angles)]) / math.sqrt(channels)
     high = table.astype(ml_dtypes.bfloat16)
     low = (table - high.astype(np.float64)).astype(ml_dtypes.bfloat16)
-    return jnp.asarray(high), jnp.asarray(low)
+    return jnp.asarray(np.stack([high, low]))
+
+
+def stage_kernel(source, out):
+    out[...] = source[...]
+
+
+def stage(table):
+    return pl.pallas_call(
+        stage_kernel,
+        out_shape=jax.ShapeDtypeStruct(table.shape, table.dtype),
+        in_specs=[VMEM],
+        out_specs=VMEM,
+        compiler_params=pltpu.CompilerParams(vmem_limit_bytes=4 * 2**20),
+        name="stage",
+    )(table)
 
 
 def pack_kernel(voltages, same, cross):
@@ -52,6 +67,7 @@
         out_shape=[jax.ShapeDtypeStruct((BATCHES, frames, samples, LANES), BF16)] * 2,
         in_specs=[VMEM],
         out_specs=[VMEM] * 2,
+        compiler_params=pltpu.CompilerParams(vmem_limit_bytes=4 * 2**20),
         name="pack",
     )(voltages)
 
@@ -71,13 +87,14 @@
         out_shape=[jax.ShapeDtypeStruct((2 * frames, samples, LANES), BF16)] * batches,
         in_specs=[VMEM] * 2,
         out_specs=[VMEM] * batches,
+        compiler_params=pltpu.CompilerParams(vmem_limit_bytes=4 * 2**20),
         name="arrange",
     )(same, cross)
 
 
 def filter_kernel(
     taps, frames, place, left, own, right,
-    coef, high, low, valid, out, held, w_high, w_low, turned, sems
+    coef, table, valid, out, held, w_high, w_low, turned, sems
 ):
     wraps = place[0]
     samples = own.shape[1]
@@ -122,9 +139,9 @@
     keep = valid[...]
     sign = jnp.where(lax.broadcasted_iota(jnp.int32, (1, LANES), 1) < HALF, 1.0, -1.0).astype(F32)
     for pair in range(frames // 2):
-        block = jnp.dot(high[...], w_high[pair], preferred_element_type=F32)
-        block += jnp.dot(high[...], w_low[pair], preferred_element_type=F32)
-        block += jnp.dot(low[...], w_high[pair], preferred_element_type=F32)
+        block = jnp.dot(table[0], w_high[pair], preferred_element_type=F32)
+        block += jnp.dot(table[0], w_low[pair], preferred_element_type=F32)
+        block += jnp.dot(table[1], w_high[pair], preferred_element_type=F32)
         for which in range(2):
             lanes = slice(which * LANES, (which + 1) * LANES)
             cosines, sines = block[:samples, lanes], block[samples:, lanes]
@@ -140,13 +157,13 @@
     lax.fori_loop(0, out.shape[0], one_dest, 0, unroll=8)
 
 
-def filter_bank(place, blocks, coef, high, low, valid, dests):
+def filter_bank(place, blocks, coef, table, valid, dests):
     samples, taps = coef.shape
     frames = blocks[0].shape[0]
     return pl.pallas_call(
         functools.partial(filter_kernel, taps, frames),
         out_shape=jax.ShapeDtypeStruct((dests, samples // dests * frames, LANES), BF16),
-        in_specs=[SMEM] + [ANY] * 3 + [VMEM] * 4,
+        in_specs=[SMEM] + [ANY] * 3 + [VMEM] * 3,
         out_specs=VMEM,
         scratch_shapes=[
             pltpu.VMEM((3 * frames, samples, LANES), BF16),
@@ -158,7 +175,7 @@
         compiler_params=pltpu.CompilerParams(vmem_limit_bytes=12 * 2**20),
         cost_estimate=pl.CostEstimate(flops=20000000000, bytes_accessed=2**20, transcendentals=0),
         name="filter_bank",
-    )(place, *blocks, coef, high, low, valid)
+    )(place, *blocks, coef, table, valid)
 
 
 def columns_of(pieces):
@@ -271,7 +288,7 @@
         halos = [(lax.ppermute(o, TIME, route(1, 0)), o, lax.ppermute(o, TIME, route(-1, 0))) for o in owns]
 
     coef = taps_coef.T
-    high, low = fourier_table(samples)
+    table = stage(fourier_table(samples))
     valid = (1 - flags).astype(F32)
 
     own_slots = lax.dynamic_slice_in_dim(station_map, row * width, width)
@@ -291,7 +308,7 @@
         flagged = lax.dynamic_slice_in_dim(valid, core * LANES + batch * HALF, HALF)
         keep = jnp.concatenate([flagged, flagged])[None, :]
         with jax.named_scope("filter"):
-            spectra = filter_bank(place, halos[batch], coef, high, low, keep, dests)
+            spectra = filter_bank(place, halos[batch], coef, table, keep, dests)
         with jax.named_scope("exchange"):
             block = lax.all_to_all(spectra, TIME, 0, 0, tiled=True)
         block = block.reshape(chips, cores, -1, LANES)
@@ -301,8 +318,8 @@
             far.append([lax.ppermute(above[:half], "inp", up), lax.ppermute(below[half:], "inp", down)])
         near += [[block], [above], [below]]
     with jax.named_scope("order"):
-        table = picks([(turn, batch) for batch in range(BATCHES) for turn in (0, 1, 3)])
-        early = order_inputs(near, table, chip_frames)
+        tables = picks([(turn, batch) for batch in range(BATCHES) for turn in (0, 1, 3)])
+        early = order_inputs(near, tables, chip_frames)
     with jax.named_scope("correlate"):
         out = correlate(far, picks([(2, batch) for batch in range(BATCHES)]), early, scale, chip_frames, shape)
     return out

time: 121 us -> 114 us (0.942)
  Pallas kernels: 25.6 us -> 21.2 us
  local copies, waits for them, and re-layouts: 4.81 us -> 3.32 us
    pallas_call x1, Pallas kernels: 2.28 us -> 0.08 us  [arrange(): pl.pallas_call(arrange_kernel, out_shape=[jax.ShapeDtypeStruct((2 * frame...]
    pallas_call x1, Pallas kernels: 2.73 us -> 0.55 us  [pack(): pl.pallas_call(pack_kernel, out_shape=[jax.ShapeDtypeStruct((BATCHES, fra...]
    unnamed x17 -> x9, local copies, waits for them, and re-layouts: 4.58 us -> 3.09 us
where the time goes in v3:
time: 114 us
  waiting for transfers between devices  50.1 us (44%)
  starting transfers between devices  37.9 us (33%)
  Pallas kernels  21.2 us (19%)
  local copies, waits for them, and re-layouts  3.32 us (3%)
    all_to_all x2, waiting for transfers between devices, local(): block = lax.all_to_all(spectra, TIME, 0, 0, tiled=True)  26.1 us
    all_to_all x2, starting transfers between devices, local(): block = lax.all_to_all(spectra, TIME, 0, 0, tiled=True)  12.4 us
    ppermute x2, starting transfers between devices, local(): lax.ppermute(o, TIME, route(-1, 0))  10.9 us
    pallas_call x2, Pallas kernels, filter_bank(): pl.pallas_call(functools.partial(filter_kernel, taps, frames), out_shape=...  9.21 us
    ppermute x2, waiting for transfers between devices, local(): lax.ppermute(block, 'inp', down)  8.3 us
    pallas_call x1, Pallas kernels, correlate(): pl.pallas_call(functools.partial(correlate_kernel, scale, counts, frames)...  6.63 us
    ppermute x2, waiting for transfers between devices, local(): lax.ppermute(o, TIME, route(-1, 0))  6.26 us
    ppermute x2, waiting for transfers between devices, local(): lax.ppermute(o, TIME, route(1, 0))  5.79 us
  transfers between devices with their start and end apart: 15, of which 7 were waited for; matrix products, arithmetic and copies ran while one was open for 2% of the time, Pallas kernels for 12%

profile of v3, /device:TPU:1, one launch (start us, length us, event | category | flops | bytes accessed | tf_op | source)
XLA Modules:
  0.0 113.8 jit_solution(17256371512855433159)
XLA Ops:
  0.0 1.2 %copy-done = bf16[4,2,256,256]{3,2,1,0:T(8,128)(2,1)S(1)} copy-done((bf16[4,2,256,256]{3,2,1,0:T(8,128)(2,1)S(1)}, bf16[4,2,256,256]{3,2,1,0:T(8,128)(2,1)}, u32[]{:S(2)}) %copy-start) | copy-done | bytes 1048600
  1.8 3.3 %collective-permute-start = (bf16[2,4,256,128]{3,2,1,0:T(8,128)(2,1)S(1)}, bf16[2,4,256,128]{3,2,1,0:T(8,128)(2,1)S(1)}, u32[]{:S(2)}, u32[]{:S(2)}) collective-permute-start(bf16[2,4,256,128]{3,2,1,0:T(8,128)(2,1)S(1)} %get-tuple-element.12), channel_id=1, source_target_pairs={{1,0},{0,1},{9,8},{8,9},{17,16},{16,17},{25,24},{24,25},{33,32},{3... | collective-permute-start | bytes 1572872 | tf_op jit(solution)/shard_map/halo/ppermute | solution.py:287
  5.1 0.8 copy.6
  5.9 1.0 copy-done.1
  7.1 6.1 %collective-permute-start.2 = (bf16[8,256,128]{2,1,0:T(8,128)(2,1)S(1)}, bf16[8,256,128]{2,1,0:T(8,128)(2,1)S(1)}, u32[]{:S(2)}, u32[]{:S(2)}) collective-permute-start(bf16[8,256,128]{2,1,0:T(8,128)(2,1)S(1)} %get-tuple-element.13.own), channel_id=1, source_target_pairs={{8,0},{9,1},{16,8},{17,9},{24,16},{25,17},{32,24},{33,25},{40,32},... | collective-permute-start | bytes 1572872 | tf_op jit(solution)/shard_map/halo/ppermute | solution.py:288
  13.5 4.8 %collective-permute-start.8 = (bf16[8,256,128]{2,1,0:T(8,128)(2,1)S(1)}, bf16[8,256,128]{2,1,0:T(8,128)(2,1)S(1)}, u32[]{:S(2)}, u32[]{:S(2)}) collective-permute-start(bf16[8,256,128]{2,1,0:T(8,128)(2,1)S(1)} %get-tuple-element.14.own), channel_id=1, source_target_pairs={{8,0},{9,1},{16,8},{17,9},{24,16},{25,17},{32,24},{33,25},{40,32},... | collective-permute-start | bytes 1572872 | tf_op jit(solution)/shard_map/halo/ppermute | solution.py:288
  18.3 6.3 %collective-permute-done.2.right = bf16[8,256,128]{2,1,0:T(8,128)(2,1)S(1)} collective-permute-done((bf16[8,256,128]{2,1,0:T(8,128)(2,1)S(1)}, bf16[8,256,128]{2,1,0:T(8,128)(2,1)S(1)}, u32[]{:S(2)}, u32[]{:S(2)}) %collective-permute-start.2) | collective-permute-done | bytes 524320 | tf_op jit(solution)/shard_map/halo/ppermute | solution.py:288
  24.5 5.2 %collective-permute-done.1.left = bf16[8,256,128]{2,1,0:T(8,128)(2,1)S(1)} collective-permute-done((bf16[8,256,128]{2,1,0:T(8,128)(2,1)S(1)}, bf16[8,256,128]{2,1,0:T(8,128)(2,1)S(1)}, u32[]{:S(2)}, u32[]{:S(2)}) %collective-permute-start.1) | collective-permute-done | bytes 524320 | tf_op jit(solution)/shard_map/halo/ppermute | solution.py:288
  29.7 4.6 %filter_bank.2 = bf16[64,32,128]{2,1,0:T(8,128)(2,1)} custom-call(s32[1]{0:T(128)} %bitcast.place, bf16[8,256,128]{2,1,0:T(8,128)(2,1)S(1)} %collective-permute-done.1.left, bf16[8,256,128]{2,1,0:T(8,128)(2,1)S(1)} %get-tuple-element.13.own, bf16[8,256,128]{2,1,0:T(8,128)(2,1)S(1)} %collective-permute-done.2.right, f32[256,16]{1,0:T(8,128)S(1)} %bitcast.14, ...), custom_call_target="tpu_custom_call" | custom-call | flops 20000000000 | bytes 1048576 | tf_op jit(solution)/shard_map/filter/filter_bank/pallas_call | solution.py:163
  34.3 6.0 %all-to-all-start = ((bf16[64,32,128]{2,1,0:T(8,128)(2,1)}), bf16[64,32,128]{2,1,0:T(8,128)(2,1)S(1)}, u32[]{:S(2)}, u32[]{:S(2)}) async-start(bf16[64,32,128]{2,1,0:T(8,128)(2,1)} %filter_bank.2), calls=%async_computation | async-start | bytes 1048576 | tf_op jit(solution)/shard_map/exchange/all_to_all | solution.py:313
  41.0 4.6 %filter_bank.3 = bf16[64,32,128]{2,1,0:T(8,128)(2,1)} custom-call(s32[1]{0:T(128)} %bitcast.place, bf16[8,256,128]{2,1,0:T(8,128)(2,1)S(1)} %collective-permute-done.7.left, bf16[8,256,128]{2,1,0:T(8,128)(2,1)S(1)} %get-tuple-element.14.own, bf16[8,256,128]{2,1,0:T(8,128)(2,1)S(1)} %collective-permute-done.8.right, f32[256,16]{1,0:T(8,128)S(1)} %bitcast.15, ...), custom_call_target="tpu_custom_call" | custom-call | flops 20000000000 | bytes 1048576 | tf_op jit(solution)/shard_map/filter/filter_bank/pallas_call | solution.py:163
  45.6 12.1 %all-to-all-done = bf16[64,32,128]{2,1,0:T(8,128)(2,1)S(1)} async-done(((bf16[64,32,128]{2,1,0:T(8,128)(2,1)}), bf16[64,32,128]{2,1,0:T(8,128)(2,1)S(1)}, u32[]{:S(2)}, u32[]{:S(2)}) %all-to-all-start) | async-done | bytes 524320 | tf_op jit(solution)/shard_map/exchange/all_to_all | solution.py:313
  57.7 6.4 %all-to-all-start.1 = ((bf16[64,32,128]{2,1,0:T(8,128)(2,1)}), bf16[64,32,128]{2,1,0:T(8,128)(2,1)S(1)}, u32[]{:S(2)}, u32[]{:S(2)}) async-start(bf16[64,32,128]{2,1,0:T(8,128)(2,1)} %filter_bank.3), calls=%async_computation.1 | async-start | bytes 1048576 | tf_op jit(solution)/shard_map/exchange/all_to_all | solution.py:313
  64.5 1.4 %collective-permute-start.5 = (bf16[32,2,32,128]{3,2,1,0:T(8,128)(2,1)S(1)}, bf16[32,2,32,128]{3,2,1,0:T(8,128)(2,1)S(1)}, u32[]{:S(2)}, u32[]{:S(2)}) collective-permute-start(bf16[32,2,32,128]{3,2,1,0:T(8,128)(2,1)S(1)} %bitcast.8), channel_id=1, source_target_pairs={{6,0},{0,2},{2,4},{4,6},{7,1},{1,3},{3,5},{5,7},{14,8},{8,10},{10,... | collective-permute-start | bytes 1572872 | tf_op jit(solution)/shard_map/gather/ppermute | solution.py:316
  65.9 1.5 %collective-permute-start.3 = (bf16[32,2,32,128]{3,2,1,0:T(8,128)(2,1)S(1)}, bf16[32,2,32,128]{3,2,1,0:T(8,128)(2,1)S(1)}, u32[]{:S(2)}, u32[]{:S(2)}) collective-permute-start(bf16[32,2,32,128]{3,2,1,0:T(8,128)(2,1)S(1)} %bitcast.9), channel_id=1, source_target_pairs={{2,0},{4,2},{6,4},{0,6},{3,1},{5,3},{7,5},{1,7},{10,8},{12,10},{14... | collective-permute-start | bytes 1572872 | tf_op jit(solution)/shard_map/gather/ppermute | solution.py:316
  67.4 14.0 %all-to-all-done.1 = bf16[64,32,128]{2,1,0:T(8,128)(2,1)S(1)} async-done(((bf16[64,32,128]{2,1,0:T(8,128)(2,1)}), bf16[64,32,128]{2,1,0:T(8,128)(2,1)S(1)}, u32[]{:S(2)}, u32[]{:S(2)}) %all-to-all-start.1) | async-done | bytes 524320 | tf_op jit(solution)/shard_map/exchange/all_to_all | solution.py:313
  81.4 1.3 %collective-permute-start.11 = (bf16[32,2,32,128]{3,2,1,0:T(8,128)(2,1)S(1)}, bf16[32,2,32,128]{3,2,1,0:T(8,128)(2,1)S(1)}, u32[]{:S(2)}, u32[]{:S(2)}) collective-permute-start(bf16[32,2,32,128]{3,2,1,0:T(8,128)(2,1)S(1)} %bitcast.11), channel_id=1, source_target_pairs={{6,0},{0,2},{2,4},{4,6},{7,1},{1,3},{3,5},{5,7},{14,8},{8,10},{10,... | collective-permute-start | bytes 1572872 | tf_op jit(solution)/shard_map/gather/ppermute | solution.py:316
  82.7 1.4 %collective-permute-start.9 = (bf16[32,2,32,128]{3,2,1,0:T(8,128)(2,1)S(1)}, bf16[32,2,32,128]{3,2,1,0:T(8,128)(2,1)S(1)}, u32[]{:S(2)}, u32[]{:S(2)}) collective-permute-start(bf16[32,2,32,128]{3,2,1,0:T(8,128)(2,1)S(1)} %bitcast.12), channel_id=1, source_target_pairs={{2,0},{4,2},{6,4},{0,6},{3,1},{5,3},{7,5},{1,7},{10,8},{12,10},{14... | collective-permute-start | bytes 1572872 | tf_op jit(solution)/shard_map/gather/ppermute | solution.py:316
  84.9 2.7 %collective-permute-start.4 = (bf16[16,2,32,128]{3,2,1,0:T(8,128)(2,1)S(1)}, bf16[16,2,32,128]{3,2,1,0:T(8,128)(2,1)S(1)}, u32[]{:S(2)}, u32[]{:S(2)}) collective-permute-start(bf16[16,2,32,128]{3,2,1,0:T(8,128)(2,1)S(1)} %slice.16), channel_id=1, source_target_pairs={{2,0},{4,2},{6,4},{0,6},{3,1},{5,3},{7,5},{1,7},{10,8},{12,10},{14... | collective-permute-start | bytes 786440 | tf_op jit(solution)/shard_map/gather/ppermute | solution.py:318
  87.6 8.3 %collective-permute-done.11.refs_5_ = bf16[32,2,32,128]{3,2,1,0:T(8,128)(2,1)S(1)} collective-permute-done((bf16[32,2,32,128]{3,2,1,0:T(8,128)(2,1)S(1)}, bf16[32,2,32,128]{3,2,1,0:T(8,128)(2,1)S(1)}, u32[]{:S(2)}, u32[]{:S(2)}) %collective-permute-start.11) | collective-permute-done | bytes 524320 | tf_op jit(solution)/shard_map/gather/ppermute | solution.py:316
  96.1 2.7 %collective-permute-start.10 = (bf16[16,2,32,128]{3,2,1,0:T(8,128)(2,1)S(1)}, bf16[16,2,32,128]{3,2,1,0:T(8,128)(2,1)S(1)}, u32[]{:S(2)}, u32[]{:S(2)}) collective-permute-start(bf16[16,2,32,128]{3,2,1,0:T(8,128)(2,1)S(1)} %slice.18), channel_id=1, source_target_pairs={{2,0},{4,2},{6,4},{0,6},{3,1},{5,3},{7,5},{1,7},{10,8},{12,10},{14... | collective-permute-start | bytes 786440 | tf_op jit(solution)/shard_map/gather/ppermute | solution.py:318
  98.8 4.7 %order_inputs.1 = (bf16[4,512,1024]{2,1,0:T(8,128)(2,1)S(1)}, bf16[4,512,512]{2,1,0:T(8,128)(2,1)S(1)}) custom-call(bf16[32,2,32,128]{3,2,1,0:T(8,128)(2,1)S(1)} %bitcast.10, bf16[32,2,32,128]{3,2,1,0:T(8,128)(2,1)S(1)} %collective-permute-done.3.refs_1_, bf16[32,2,32,128]{3,2,1,0:T(8,128)(2,1)S(1)} %collective-permute-done.5.refs_2_, ...), custom_call_target="tpu_custom_call" | custom-call | flops 4026531840 | bytes 1048576 | tf_op jit(solution)/shard_map/order/order_inputs/pallas_call | solution.py:229
  103.5 3.6 %collective-permute-done.12.refs_3_ = bf16[16,2,32,128]{3,2,1,0:T(8,128)(2,1)S(1)} collective-permute-done((bf16[16,2,32,128]{3,2,1,0:T(8,128)(2,1)S(1)}, bf16[16,2,32,128]{3,2,1,0:T(8,128)(2,1)S(1)}, u32[]{:S(2)}, u32[]{:S(2)}) %collective-permute-start.12) | collective-permute-done | bytes 262176 | tf_op jit(solution)/shard_map/gather/ppermute | solution.py:318
  107.2 6.6 %correlate.1 = f32[4,2,256,1024]{3,2,1,0:T(8,128)} custom-call(bf16[16,2,32,128]{3,2,1,0:T(8,128)(2,1)S(1)} %collective-permute-done.4.refs_0_, bf16[16,2,32,128]{3,2,1,0:T(8,128)(2,1)S(1)} %collective-permute-done.6.refs_1_, bf16[16,2,32,128]{3,2,1,0:T(8,128)(2,1)S(1)} %collective-permute-done.10.refs_2_, ...), custom_call_target="tpu_custom_call" | custom-call | tf_op jit(solution)/shard_map/correlate/correlate/pallas_call | solution.py:261
  (44 shorter events, 2.7 us)
Async XLA Ops:
  0.0 1.2 %copy-start = (bf16[4,2,256,256]{3,2,1,0:T(8,128)(2,1)S(1)}, bf16[4,2,256,256]{3,2,1,0:T(8,128)(2,1)}, u32[]{:S(2)}) copy-start(bf16[4,2,256,256]{3,2,1,0:T(8,128)(2,1)} %voltages.1) | copy-start | bytes 3145732
  1.2 12.0 %copy-start.3 = (s32[256]{0:T(256)S(1)}, s32[256]{0:T(256)}, u32[]{:S(2)}) copy-start(s32[256]{0:T(256)} %param.8) | copy-start | bytes 3076
  1.8 5.2 %collective-permute-start = (bf16[2,4,256,128]{3,2,1,0:T(8,128)(2,1)S(1)}, bf16[2,4,256,128]{3,2,1,0:T(8,128)(2,1)S(1)}, u32[]{:S(2)}, u32[]{:S(2)}) collective-permute-start(bf16[2,4,256,128]{3,2,1,0:T(8,128)(2,1)S(1)} %get-tuple-element.12), channel_id=1, source_target_pairs={{1,0},{0,1},{9,8},{8,9},{17,16},{16,17},{25,24},{24,25},{33,32},{3... | collective-permute-start | bytes 1572872 | tf_op jit(solution)/shard_map/halo/ppermute | solution.py:287
  5.9 1.0 copy-start.1
  7.1 17.4 %collective-permute-start.2 = (bf16[8,256,128]{2,1,0:T(8,128)(2,1)S(1)}, bf16[8,256,128]{2,1,0:T(8,128)(2,1)S(1)}, u32[]{:S(2)}, u32[]{:S(2)}) collective-permute-start(bf16[8,256,128]{2,1,0:T(8,128)(2,1)S(1)} %get-tuple-element.13.own), channel_id=1, source_target_pairs={{8,0},{9,1},{16,8},{17,9},{24,16},{25,17},{32,24},{33,25},{40,32},... | collective-permute-start | bytes 1572872 | tf_op jit(solution)/shard_map/halo/ppermute | solution.py:288
  13.2 16.5 %collective-permute-start.1 = (bf16[8,256,128]{2,1,0:T(8,128)(2,1)S(1)}, bf16[8,256,128]{2,1,0:T(8,128)(2,1)S(1)}, u32[]{:S(2)}, u32[]{:S(2)}) collective-permute-start(bf16[8,256,128]{2,1,0:T(8,128)(2,1)S(1)} %get-tuple-element.13.own), channel_id=1, source_target_pairs={{248,0},{249,1},{0,8},{1,9},{8,16},{9,17},{16,24},{17,25},{24,32},... | collective-permute-start | bytes 1572872 | tf_op jit(solution)/shard_map/halo/ppermute | solution.py:288
  13.5 26.9 %collective-permute-start.8 = (bf16[8,256,128]{2,1,0:T(8,128)(2,1)S(1)}, bf16[8,256,128]{2,1,0:T(8,128)(2,1)S(1)}, u32[]{:S(2)}, u32[]{:S(2)}) collective-permute-start(bf16[8,256,128]{2,1,0:T(8,128)(2,1)S(1)} %get-tuple-element.14.own), channel_id=1, source_target_pairs={{8,0},{9,1},{16,8},{17,9},{24,16},{25,17},{32,24},{33,25},{40,32},... | collective-permute-start | bytes 1572872 | tf_op jit(solution)/shard_map/halo/ppermute | solution.py:288
  18.3 22.7 %collective-permute-start.7 = (bf16[8,256,128]{2,1,0:T(8,128)(2,1)S(1)}, bf16[8,256,128]{2,1,0:T(8,128)(2,1)S(1)}, u32[]{:S(2)}, u32[]{:S(2)}) collective-permute-start(bf16[8,256,128]{2,1,0:T(8,128)(2,1)S(1)} %get-tuple-element.14.own), channel_id=1, source_target_pairs={{248,0},{249,1},{0,8},{1,9},{8,16},{9,17},{16,24},{17,25},{24,32},... | collective-permute-start | bytes 1572872 | tf_op jit(solution)/shard_map/halo/ppermute | solution.py:288
  34.3 23.4 %all-to-all-start = ((bf16[64,32,128]{2,1,0:T(8,128)(2,1)}), bf16[64,32,128]{2,1,0:T(8,128)(2,1)S(1)}, u32[]{:S(2)}, u32[]{:S(2)}) async-start(bf16[64,32,128]{2,1,0:T(8,128)(2,1)} %filter_bank.2), calls=%async_computation | async-start | bytes 1048576 | tf_op jit(solution)/shard_map/exchange/all_to_all | solution.py:313
  40.4 23.8 %copy-start.2 = (s32[1024]{0:T(1024)S(1)}, s32[1024]{0:T(1024)}, u32[]{:S(2)}) copy-start(s32[1024]{0:T(1024)} %param.7) | copy-start | bytes 12292
  57.7 23.7 %all-to-all-start.1 = ((bf16[64,32,128]{2,1,0:T(8,128)(2,1)}), bf16[64,32,128]{2,1,0:T(8,128)(2,1)S(1)}, u32[]{:S(2)}, u32[]{:S(2)}) async-start(bf16[64,32,128]{2,1,0:T(8,128)(2,1)} %filter_bank.3), calls=%async_computation.1 | async-start | bytes 1048576 | tf_op jit(solution)/shard_map/exchange/all_to_all | solution.py:313
  64.5 20.2 %collective-permute-start.5 = (bf16[32,2,32,128]{3,2,1,0:T(8,128)(2,1)S(1)}, bf16[32,2,32,128]{3,2,1,0:T(8,128)(2,1)S(1)}, u32[]{:S(2)}, u32[]{:S(2)}) collective-permute-start(bf16[32,2,32,128]{3,2,1,0:T(8,128)(2,1)S(1)} %bitcast.8), channel_id=1, source_target_pairs={{6,0},{0,2},{2,4},{4,6},{7,1},{1,3},{3,5},{5,7},{14,8},{8,10},{10,... | collective-permute-start | bytes 1572872 | tf_op jit(solution)/shard_map/gather/ppermute | solution.py:316
  65.9 19.0 %collective-permute-start.3 = (bf16[32,2,32,128]{3,2,1,0:T(8,128)(2,1)S(1)}, bf16[32,2,32,128]{3,2,1,0:T(8,128)(2,1)S(1)}, u32[]{:S(2)}, u32[]{:S(2)}) collective-permute-start(bf16[32,2,32,128]{3,2,1,0:T(8,128)(2,1)S(1)} %bitcast.9), channel_id=1, source_target_pairs={{2,0},{4,2},{6,4},{0,6},{3,1},{5,3},{7,5},{1,7},{10,8},{12,10},{14... | collective-permute-start | bytes 1572872 | tf_op jit(solution)/shard_map/gather/ppermute | solution.py:316
  81.4 14.5 %collective-permute-start.11 = (bf16[32,2,32,128]{3,2,1,0:T(8,128)(2,1)S(1)}, bf16[32,2,32,128]{3,2,1,0:T(8,128)(2,1)S(1)}, u32[]{:S(2)}, u32[]{:S(2)}) collective-permute-start(bf16[32,2,32,128]{3,2,1,0:T(8,128)(2,1)S(1)} %bitcast.11), channel_id=1, source_target_pairs={{6,0},{0,2},{2,4},{4,6},{7,1},{1,3},{3,5},{5,7},{14,8},{8,10},{10,... | collective-permute-start | bytes 1572872 | tf_op jit(solution)/shard_map/gather/ppermute | solution.py:316
  82.7 13.3 %collective-permute-start.9 = (bf16[32,2,32,128]{3,2,1,0:T(8,128)(2,1)S(1)}, bf16[32,2,32,128]{3,2,1,0:T(8,128)(2,1)S(1)}, u32[]{:S(2)}, u32[]{:S(2)}) collective-permute-start(bf16[32,2,32,128]{3,2,1,0:T(8,128)(2,1)S(1)} %bitcast.12), channel_id=1, source_target_pairs={{2,0},{4,2},{6,4},{0,6},{3,1},{5,3},{7,5},{1,7},{10,8},{12,10},{14... | collective-permute-start | bytes 1572872 | tf_op jit(solution)/shard_map/gather/ppermute | solution.py:316
  84.8 18.7 %collective-permute-start.6 = (bf16[16,2,32,128]{3,2,1,0:T(8,128)(2,1)S(1)}, bf16[16,2,32,128]{3,2,1,0:T(8,128)(2,1)S(1)}, u32[]{:S(2)}, u32[]{:S(2)}) collective-permute-start(bf16[16,2,32,128]{3,2,1,0:T(8,128)(2,1)S(1)} %slice.17), channel_id=1, source_target_pairs={{6,0},{0,2},{2,4},{4,6},{7,1},{1,3},{3,5},{5,7},{14,8},{8,10},{10,... | collective-permute-start | bytes 786440 | tf_op jit(solution)/shard_map/gather/ppermute | solution.py:318
  84.9 18.6 %collective-permute-start.4 = (bf16[16,2,32,128]{3,2,1,0:T(8,128)(2,1)S(1)}, bf16[16,2,32,128]{3,2,1,0:T(8,128)(2,1)S(1)}, u32[]{:S(2)}, u32[]{:S(2)}) collective-permute-start(bf16[16,2,32,128]{3,2,1,0:T(8,128)(2,1)S(1)} %slice.16), channel_id=1, source_target_pairs={{2,0},{4,2},{6,4},{0,6},{3,1},{5,3},{7,5},{1,7},{10,8},{12,10},{14... | collective-permute-start | bytes 786440 | tf_op jit(solution)/shard_map/gather/ppermute | solution.py:318
  96.0 11.2 %collective-permute-start.12 = (bf16[16,2,32,128]{3,2,1,0:T(8,128)(2,1)S(1)}, bf16[16,2,32,128]{3,2,1,0:T(8,128)(2,1)S(1)}, u32[]{:S(2)}, u32[]{:S(2)}) collective-permute-start(bf16[16,2,32,128]{3,2,1,0:T(8,128)(2,1)S(1)} %slice.19), channel_id=1, source_target_pairs={{6,0},{0,2},{2,4},{4,6},{7,1},{1,3},{3,5},{5,7},{14,8},{8,10},{10,... | collective-permute-start | bytes 786440 | tf_op jit(solution)/shard_map/gather/ppermute | solution.py:318
  96.1 11.1 %collective-permute-start.10 = (bf16[16,2,32,128]{3,2,1,0:T(8,128)(2,1)S(1)}, bf16[16,2,32,128]{3,2,1,0:T(8,128)(2,1)S(1)}, u32[]{:S(2)}, u32[]{:S(2)}) collective-permute-start(bf16[16,2,32,128]{3,2,1,0:T(8,128)(2,1)S(1)} %slice.18), channel_id=1, source_target_pairs={{2,0},{4,2},{6,4},{0,6},{3,1},{5,3},{7,5},{1,7},{10,8},{12,10},{14... | collective-permute-start | bytes 786440 | tf_op jit(solution)/shard_map/gather/ppermute | solution.py:318

commit v4 on v3

--- a/solution.py
+++ b/solution.py
@@ -209,7 +209,14 @@
 
 
 def grouped(refs, counts):
-    return [refs[sum(counts[:n]) :][:count] for n, count in enumerate(counts)]
+    blocks = []
+    for n, count in enumerate(counts):
+        group = refs[sum(counts[:n]) :][:count]
+        if len(group[0].shape) > 4:
+            blocks += [[group[0].at[row]] for row in range(group[0].shape[0])]
+        else:
+            blocks.append(group)
+    return blocks
 
 
 def order_kernel(counts, frames, *refs):
@@ -222,8 +229,8 @@
 def order_inputs(blocks, picks, frames):
     counts = [len(b) for b in blocks]
     operands = [piece for b in blocks for piece in b] + [*picks]
-    channels = blocks[0][0].shape[2] // frames
-    depth = 2 * frames * sum(p.shape[0] for p in blocks[0])
+    channels = blocks[-1][0].shape[2] // frames
+    depth = 2 * frames * sum(p.shape[0] for p in blocks[-1])
     shapes = [(channels, depth, picks[0].shape[1]), (channels, depth, 2 * picks[1].shape[1])]
     flops = 2 * channels * depth * picks[0].shape[0] * (picks[0].shape[1] + picks[1].shape[1])
     return pl.pallas_call(
@@ -295,7 +302,7 @@
 
     def picks(blocks):
         at = jnp.arange(LANES, dtype=jnp.int32)
-        held = [(row + turn) % rows * width + at // HALF * LANES + batch * HALF + at % HALF for turn, batch in blocks]
+        held = [source * width + at // HALF * LANES + batch * HALF + at % HALF for source, batch in blocks]
         held = jnp.concatenate(held)
         return [(held[:, None] == slots[None, :]).astype(BF16) for slots in (station_map, own_slots)]
 
@@ -303,25 +310,34 @@
     down = [((i - 1) % rows, i) for i in range(rows)]
     shape = (samples // dests, 2, width, inputs)
     scale = 1.0 / (frames * dests)
-    near, far = [], []
+    near, sources = [], []
+    spectra = []
     for batch in range(BATCHES):
         flagged = lax.dynamic_slice_in_dim(valid, core * LANES + batch * HALF, HALF)
         keep = jnp.concatenate([flagged, flagged])[None, :]
         with jax.named_scope("filter"):
-            spectra = filter_bank(place, halos[batch], coef, table, keep, dests)
+            spectrum = filter_bank(place, halos[batch], coef, table, keep, dests)
+        spectra.append(spectrum)
+    for batch in range(BATCHES):
         with jax.named_scope("exchange"):
-            block = lax.all_to_all(spectra, TIME, 0, 0, tiled=True)
+            block = lax.all_to_all(spectra[batch], TIME, 0, 0, tiled=True)
+            if batch < BATCHES - 1:
+                block, spectra[batch + 1] = lax.optimization_barrier((block, spectra[batch + 1]))
         block = block.reshape(chips, cores, -1, LANES)
         with jax.named_scope("gather"):
+            if batch < BATCHES - 1:
+                near.append([lax.all_gather(block, "inp", axis=0)])
+                sources += [(source, batch) for source in range(rows)]
+                continue
             above, below = lax.ppermute(block, "inp", up), lax.ppermute(block, "inp", down)
             half = chips // 2
-            far.append([lax.ppermute(above[:half], "inp", up), lax.ppermute(below[half:], "inp", down)])
-        near += [[block], [above], [below]]
+            far = [lax.ppermute(above[:half], "inp", up), lax.ppermute(below[half:], "inp", down)]
+            near += [[block], [above], [below]]
+            sources += [((row + turn) % rows, batch) for turn in (0, 1, 3)]
     with jax.named_scope("order"):
-        tables = picks([(turn, batch) for batch in range(BATCHES) for turn in (0, 1, 3)])
-        early = order_inputs(near, tables, chip_frames)
+        early = order_inputs(near, picks(sources), chip_frames)
     with jax.named_scope("correlate"):
-        out = correlate(far, picks([(2, batch) for batch in range(BATCHES)]), early, scale, chip_frames, shape)
+        out = correlate([far], picks([((row + 2) % rows, BATCHES - 1)]), early, scale, chip_frames, shape)
     return out
 
 

time: 114 us -> 136 us (1.19)
  between operations: 0.29 us -> 13.7 us
  local copies, waits for them, and re-layouts: 3.32 us -> 9.51 us
  starting transfers between devices: 37.9 us -> 31.9 us
  waiting for transfers between devices: 50.1 us -> 55 us
  Pallas kernels: 21.2 us -> 23.4 us
    ppermute x2 -> x1, waiting for transfers between devices: 8.3 us -> 14.6 us  [local(): lax.ppermute(block, 'inp', down)]
    unnamed x9 -> x19, local copies, waits for them, and re-layouts: 3.09 us -> 7.81 us
    ppermute x2 -> x1, waiting for transfers between devices: 3.63 us -> 0.01 us  [local(): lax.ppermute(below[half:], 'inp', down)]
    ppermute x2 -> x1, starting transfers between devices: 5.46 us -> 2.54 us  [local(): lax.ppermute(above[:half], 'inp', up)]
    all_to_all x2, waiting for transfers between devices: 26.1 us -> 29 us  [local(): block = lax.all_to_all(spectra[batch], TIME, 0, 0, tiled=True)]
    ppermute x2 -> x1, starting transfers between devices: 2.97 us -> 1.44 us  [local(): lax.ppermute(block, 'inp', up)]
    ppermute x2 -> x1, starting transfers between devices: 2.67 us -> 1.3 us  [local(): lax.ppermute(block, 'inp', down)]
  transfers between devices with their start and end apart: 15 -> 12, of which waited for: 7 -> 6; matrix products, arithmetic and copies ran while one was open for 2% -> 3% of each run, Pallas kernels for 12% -> 11%
where the time goes in v4:
time: 136 us; the launch traced here: 135 us
  waiting for transfers between devices  55 us (40%)
  starting transfers between devices  31.9 us (23%)
  Pallas kernels  23.4 us (17%)
  between operations  13.7 us (10%)
  local copies, waits for them, and re-layouts  9.51 us (7%)
  other arithmetic  1.66 us (1%)
    all_to_all x2, waiting for transfers between devices, local(): block = lax.all_to_all(spectra[batch], TIME, 0, 0, tiled=True)  29 us
    ppermute x1, waiting for transfers between devices, local(): lax.ppermute(block, 'inp', down)  14.6 us
    all_to_all x2, starting transfers between devices, local(): block = lax.all_to_all(spectra[batch], TIME, 0, 0, tiled=True)  12.3 us
    ppermute x2, starting transfers between devices, local(): lax.ppermute(o, TIME, route(-1, 0))  10.9 us
    pallas_call x2, Pallas kernels, filter_bank(): pl.pallas_call(functools.partial(filter_kernel, taps, frames), out_shape=...  9.22 us
    unnamed x19, local copies, waits for them, and re-layouts  7.81 us
    pallas_call x1, Pallas kernels, correlate(): pl.pallas_call(functools.partial(correlate_kernel, scale, counts, frames)...  7.46 us
    pallas_call x1, Pallas kernels, order_inputs(): pl.pallas_call(functools.partial(order_kernel, counts, frames), out_shape...  6.02 us
  transfers between devices with their start and end apart: 12, of which 6 were waited for; matrix products, arithmetic and copies ran while one was open for 3% of the time, Pallas kernels for 11%

profile of v4, /device:TPU:1, one launch (start us, length us, event | category | flops | bytes accessed | tf_op | source)
XLA Modules:
  0.0 135.0 jit_solution(12038949220944998408)
XLA Ops:
  6.5 1.2 copy-done
  8.3 3.3 %collective-permute-start = (bf16[2,4,256,128]{3,2,1,0:T(8,128)(2,1)S(1)}, bf16[2,4,256,128]{3,2,1,0:T(8,128)(2,1)S(1)}, u32[]{:S(2)}, u32[]{:S(2)}) collective-permute-start(bf16[2,4,256,128]{3,2,1,0:T(8,128)(2,1)S(1)} %get-tuple-element.14), channel_id=1, source_target_pairs={{1,0},{0,1},{9,8},{8,9},{17,16},{16,17},{25,24},{24,25},{33,32},{3... | collective-permute-start | bytes 1572872 | tf_op jit(solution)/shard_map/halo/ppermute | solution.py:294
  11.7 0.8 copy.7
  12.5 1.0 copy-done.1
  13.7 6.1 %collective-permute-start.2 = (bf16[8,256,128]{2,1,0:T(8,128)(2,1)S(1)}, bf16[8,256,128]{2,1,0:T(8,128)(2,1)S(1)}, u32[]{:S(2)}, u32[]{:S(2)}) collective-permute-start(bf16[8,256,128]{2,1,0:T(8,128)(2,1)S(1)} %get-tuple-element.15.own), channel_id=1, source_target_pairs={{8,0},{9,1},{16,8},{17,9},{24,16},{25,17},{32,24},{33,25},{40,32},... | collective-permute-start | bytes 1572872 | tf_op jit(solution)/shard_map/halo/ppermute | solution.py:295
  20.7 4.8 %collective-permute-start.4 = (bf16[8,256,128]{2,1,0:T(8,128)(2,1)S(1)}, bf16[8,256,128]{2,1,0:T(8,128)(2,1)S(1)}, u32[]{:S(2)}, u32[]{:S(2)}) collective-permute-start(bf16[8,256,128]{2,1,0:T(8,128)(2,1)S(1)} %get-tuple-element.16.own), channel_id=1, source_target_pairs={{8,0},{9,1},{16,8},{17,9},{24,16},{25,17},{32,24},{33,25},{40,32},... | collective-permute-start | bytes 1572872 | tf_op jit(solution)/shard_map/halo/ppermute | solution.py:295
  25.5 5.6 %collective-permute-done.2.right = bf16[8,256,128]{2,1,0:T(8,128)(2,1)S(1)} collective-permute-done((bf16[8,256,128]{2,1,0:T(8,128)(2,1)S(1)}, bf16[8,256,128]{2,1,0:T(8,128)(2,1)S(1)}, u32[]{:S(2)}, u32[]{:S(2)}) %collective-permute-start.2) | collective-permute-done | bytes 524320 | tf_op jit(solution)/shard_map/halo/ppermute | solution.py:295
  31.1 5.2 %collective-permute-done.1.left = bf16[8,256,128]{2,1,0:T(8,128)(2,1)S(1)} collective-permute-done((bf16[8,256,128]{2,1,0:T(8,128)(2,1)S(1)}, bf16[8,256,128]{2,1,0:T(8,128)(2,1)S(1)}, u32[]{:S(2)}, u32[]{:S(2)}) %collective-permute-start.1) | collective-permute-done | bytes 524320 | tf_op jit(solution)/shard_map/halo/ppermute | solution.py:295
  36.3 4.6 %filter_bank.2 = bf16[64,32,128]{2,1,0:T(8,128)(2,1)} custom-call(s32[1]{0:T(128)} %bitcast.place, bf16[8,256,128]{2,1,0:T(8,128)(2,1)S(1)} %collective-permute-done.1.left, bf16[8,256,128]{2,1,0:T(8,128)(2,1)S(1)} %get-tuple-element.15.own, bf16[8,256,128]{2,1,0:T(8,128)(2,1)S(1)} %collective-permute-done.2.right, f32[256,16]{1,0:T(8,128)S(1)} %bitcast.11, ...), custom_call_target="tpu_custom_call" | custom-call | flops 20000000000 | bytes 1048576 | tf_op jit(solution)/shard_map/filter/filter_bank/pallas_call | solution.py:163
  40.9 5.9 %all-to-all-start = ((bf16[64,32,128]{2,1,0:T(8,128)(2,1)}), bf16[64,32,128]{2,1,0:T(8,128)(2,1)S(1)}, u32[]{:S(2)}, u32[]{:S(2)}) async-start(bf16[64,32,128]{2,1,0:T(8,128)(2,1)} %filter_bank.2), calls=%async_computation | async-start | bytes 1048576 | tf_op jit(solution)/shard_map/exchange/all_to_all | solution.py:323
  47.5 4.6 %filter_bank.3 = bf16[64,32,128]{2,1,0:T(8,128)(2,1)} custom-call(s32[1]{0:T(128)} %bitcast.place, bf16[8,256,128]{2,1,0:T(8,128)(2,1)S(1)} %collective-permute-done.3.left, bf16[8,256,128]{2,1,0:T(8,128)(2,1)S(1)} %get-tuple-element.16.own, bf16[8,256,128]{2,1,0:T(8,128)(2,1)S(1)} %collective-permute-done.4.right, f32[256,16]{1,0:T(8,128)S(1)} %bitcast.12, ...), custom_call_target="tpu_custom_call" | custom-call | flops 20000000000 | bytes 1048576 | tf_op jit(solution)/shard_map/filter/filter_bank/pallas_call | solution.py:163
  52.1 12.1 %all-to-all-done = bf16[64,32,128]{2,1,0:T(8,128)(2,1)S(1)} async-done(((bf16[64,32,128]{2,1,0:T(8,128)(2,1)}), bf16[64,32,128]{2,1,0:T(8,128)(2,1)S(1)}, u32[]{:S(2)}, u32[]{:S(2)}) %all-to-all-start) | async-done | bytes 524320 | tf_op jit(solution)/shard_map/exchange/all_to_all | solution.py:323
  64.2 0.8 copy-done.7
  65.1 6.4 %all-to-all-start.1 = ((bf16[64,32,128]{2,1,0:T(8,128)(2,1)}), bf16[64,32,128]{2,1,0:T(8,128)(2,1)S(1)}, u32[]{:S(2)}, u32[]{:S(2)}) async-start(bf16[64,32,128]{2,1,0:T(8,128)(2,1)} %filter_bank.3), calls=%async_computation.1 | async-start | bytes 1048576 | tf_op jit(solution)/shard_map/exchange/all_to_all | solution.py:323
  71.9 16.9 %all-to-all-done.1 = bf16[64,32,128]{2,1,0:T(8,128)(2,1)S(1)} async-done(((bf16[64,32,128]{2,1,0:T(8,128)(2,1)}), bf16[64,32,128]{2,1,0:T(8,128)(2,1)S(1)}, u32[]{:S(2)}, u32[]{:S(2)}) %all-to-all-start.1) | async-done | bytes 524320 | tf_op jit(solution)/shard_map/exchange/all_to_all | solution.py:323
  88.8 1.3 collective-permute-start.7
  90.1 1.4 %collective-permute-start.5 = (bf16[32,2,32,128]{3,2,1,0:T(8,128)(2,1)S(1)}, bf16[32,2,32,128]{3,2,1,0:T(8,128)(2,1)S(1)}, u32[]{:S(2)}, u32[]{:S(2)}) collective-permute-start(bf16[32,2,32,128]{3,2,1,0:T(8,128)(2,1)S(1)} %bitcast.9), channel_id=1, source_target_pairs={{2,0},{4,2},{6,4},{0,6},{3,1},{5,3},{7,5},{1,7},{10,8},{12,10},{14... | collective-permute-start | bytes 1572872 | tf_op jit(solution)/shard_map/gather/ppermute | solution.py:332
  92.1 14.6 %collective-permute-done.7.refs_3_ = bf16[32,2,32,128]{3,2,1,0:T(8,128)(2,1)S(1)} collective-permute-done((bf16[32,2,32,128]{3,2,1,0:T(8,128)(2,1)S(1)}, bf16[32,2,32,128]{3,2,1,0:T(8,128)(2,1)S(1)}, u32[]{:S(2)}, u32[]{:S(2)}) %collective-permute-start.7) | collective-permute-done | bytes 524320 | tf_op jit(solution)/shard_map/gather/ppermute | solution.py:332
  108.5 2.5 %collective-permute-start.6 = (bf16[16,2,32,128]{3,2,1,0:T(8,128)(2,1)}, bf16[16,2,32,128]{3,2,1,0:T(8,128)(2,1)}, u32[]{:S(2)}, u32[]{:S(2)}) collective-permute-start(bf16[16,2,32,128]{3,2,1,0:T(8,128)(2,1)} %slice.8), channel_id=1, source_target_pairs={{2,0},{4,2},{6,4},{0,6},{3,1},{5,3},{7,5},{1,7},{10,8},{12,10},{14... | collective-permute-start | bytes 786440 | tf_op jit(solution)/shard_map/gather/ppermute | solution.py:334
  111.0 1.0 copy-done.3
  112.1 1.0 copy-done.5
  113.1 1.6 %copy-done.6 = bf16[4,32,2,32,128]{4,3,2,1,0:T(8,128)(2,1)S(1)} copy-done((bf16[4,32,2,32,128]{4,3,2,1,0:T(8,128)(2,1)S(1)}, bf16[4,32,2,32,128]{4,3,2,1,0:T(8,128)(2,1)}, u32[]{:S(2)}) %copy-start.6) | copy-done | bytes 2097176
  114.7 6.0 %order_inputs.1 = (bf16[4,512,1024]{2,1,0:T(8,128)(2,1)S(1)}, bf16[4,512,512]{2,1,0:T(8,128)(2,1)S(1)}) custom-call(bf16[4,32,2,32,128]{4,3,2,1,0:T(8,128)(2,1)S(1)} %copy-done.6, bf16[32,2,32,128]{3,2,1,0:T(8,128)(2,1)S(1)} %bitcast.10, bf16[32,2,32,128]{3,2,1,0:T(8,128)(2,1)S(1)} %copy-done.5, bf16[32,2,32,128]{3,2,1,0:T(8,128)(2,1)S(1)} %copy-done.3, ...), custom_call_target="tpu_custom_call" | custom-call | flops 4697620480 | bytes 1048576 | tf_op jit(solution)/shard_map/order/order_inputs/pallas_call | solution.py:236
  120.7 7.5 %correlate.1 = f32[4,2,256,1024]{3,2,1,0:T(8,128)} custom-call(bf16[16,2,32,128]{3,2,1,0:T(8,128)(2,1)} %collective-permute-done.6.refs_0_, bf16[16,2,32,128]{3,2,1,0:T(8,128)(2,1)S(1)} %collective-permute-done.8.refs_1_, bf16[128,1024]{1,0:T(8,128)(2,1)S(1)} %compare_convert_fusion.2.refs_2_, bf16[128,256]{1,0:T(8,128)(2,1)S(1)} %compare_convert_fusion.3.refs_3_, ...), custom_call_target="tpu_custom_call" | custom-call | tf_op jit(solution)/shard_map/correlate/correlate/pallas_call | solution.py:268
  (47 shorter events, 5.0 us)
Async XLA Ops:
  6.5 1.2 copy-start
  8.3 5.2 %collective-permute-start = (bf16[2,4,256,128]{3,2,1,0:T(8,128)(2,1)S(1)}, bf16[2,4,256,128]{3,2,1,0:T(8,128)(2,1)S(1)}, u32[]{:S(2)}, u32[]{:S(2)}) collective-permute-start(bf16[2,4,256,128]{3,2,1,0:T(8,128)(2,1)S(1)} %get-tuple-element.14), channel_id=1, source_target_pairs={{1,0},{0,1},{9,8},{8,9},{17,16},{16,17},{25,24},{24,25},{33,32},{3... | collective-permute-start | bytes 1572872 | tf_op jit(solution)/shard_map/halo/ppermute | solution.py:294
  12.5 1.0 copy-start.1
  13.7 17.4 %collective-permute-start.2 = (bf16[8,256,128]{2,1,0:T(8,128)(2,1)S(1)}, bf16[8,256,128]{2,1,0:T(8,128)(2,1)S(1)}, u32[]{:S(2)}, u32[]{:S(2)}) collective-permute-start(bf16[8,256,128]{2,1,0:T(8,128)(2,1)S(1)} %get-tuple-element.15.own), channel_id=1, source_target_pairs={{8,0},{9,1},{16,8},{17,9},{24,16},{25,17},{32,24},{33,25},{40,32},... | collective-permute-start | bytes 1572872 | tf_op jit(solution)/shard_map/halo/ppermute | solution.py:295
  19.8 16.5 %collective-permute-start.1 = (bf16[8,256,128]{2,1,0:T(8,128)(2,1)S(1)}, bf16[8,256,128]{2,1,0:T(8,128)(2,1)S(1)}, u32[]{:S(2)}, u32[]{:S(2)}) collective-permute-start(bf16[8,256,128]{2,1,0:T(8,128)(2,1)S(1)} %get-tuple-element.15.own), channel_id=1, source_target_pairs={{248,0},{249,1},{0,8},{1,9},{8,16},{9,17},{16,24},{17,25},{24,32},... | collective-permute-start | bytes 1572872 | tf_op jit(solution)/shard_map/halo/ppermute | solution.py:295
  20.7 26.2 %collective-permute-start.4 = (bf16[8,256,128]{2,1,0:T(8,128)(2,1)S(1)}, bf16[8,256,128]{2,1,0:T(8,128)(2,1)S(1)}, u32[]{:S(2)}, u32[]{:S(2)}) collective-permute-start(bf16[8,256,128]{2,1,0:T(8,128)(2,1)S(1)} %get-tuple-element.16.own), channel_id=1, source_target_pairs={{8,0},{9,1},{16,8},{17,9},{24,16},{25,17},{32,24},{33,25},{40,32},... | collective-permute-start | bytes 1572872 | tf_op jit(solution)/shard_map/halo/ppermute | solution.py:295
  25.5 22.1 %collective-permute-start.3 = (bf16[8,256,128]{2,1,0:T(8,128)(2,1)S(1)}, bf16[8,256,128]{2,1,0:T(8,128)(2,1)S(1)}, u32[]{:S(2)}, u32[]{:S(2)}) collective-permute-start(bf16[8,256,128]{2,1,0:T(8,128)(2,1)S(1)} %get-tuple-element.16.own), channel_id=1, source_target_pairs={{248,0},{249,1},{0,8},{1,9},{8,16},{9,17},{16,24},{17,25},{24,32},... | collective-permute-start | bytes 1572872 | tf_op jit(solution)/shard_map/halo/ppermute | solution.py:295
  40.9 23.3 %all-to-all-start = ((bf16[64,32,128]{2,1,0:T(8,128)(2,1)}), bf16[64,32,128]{2,1,0:T(8,128)(2,1)S(1)}, u32[]{:S(2)}, u32[]{:S(2)}) async-start(bf16[64,32,128]{2,1,0:T(8,128)(2,1)} %filter_bank.2), calls=%async_computation | async-start | bytes 1048576 | tf_op jit(solution)/shard_map/exchange/all_to_all | solution.py:323
  46.9 24.7 %copy-start.8 = (s32[1024]{0:T(1024)S(1)}, s32[1024]{0:T(1024)}, u32[]{:S(2)}) copy-start(s32[1024]{0:T(1024)} %param.7) | copy-start | bytes 12292
  46.9 64.1 %all-gather.2.cloned.1.call-start = ((), (), s32[]{:S(2)}) async-start(), calls=%async_computation.2 | async-start | bytes 2621440 | tf_op jit(solution)/shard_map/gather/all_gather | solution.py:329
  64.2 0.8 copy-start.7
  65.1 23.7 %all-to-all-start.1 = ((bf16[64,32,128]{2,1,0:T(8,128)(2,1)}), bf16[64,32,128]{2,1,0:T(8,128)(2,1)S(1)}, u32[]{:S(2)}, u32[]{:S(2)}) async-start(bf16[64,32,128]{2,1,0:T(8,128)(2,1)} %filter_bank.3), calls=%async_computation.1 | async-start | bytes 1048576 | tf_op jit(solution)/shard_map/exchange/all_to_all | solution.py:323
  88.8 17.9 %collective-permute-start.7 = (bf16[32,2,32,128]{3,2,1,0:T(8,128)(2,1)S(1)}, bf16[32,2,32,128]{3,2,1,0:T(8,128)(2,1)S(1)}, u32[]{:S(2)}, u32[]{:S(2)}) collective-permute-start(bf16[32,2,32,128]{3,2,1,0:T(8,128)(2,1)S(1)} %bitcast.8), channel_id=1, source_target_pairs={{6,0},{0,2},{2,4},{4,6},{7,1},{1,3},{3,5},{5,7},{14,8},{8,10},{10,... | collective-permute-start | bytes 1572872 | tf_op jit(solution)/shard_map/gather/ppermute | solution.py:332
  90.1 17.4 %collective-permute-start.5 = (bf16[32,2,32,128]{3,2,1,0:T(8,128)(2,1)S(1)}, bf16[32,2,32,128]{3,2,1,0:T(8,128)(2,1)S(1)}, u32[]{:S(2)}, u32[]{:S(2)}) collective-permute-start(bf16[32,2,32,128]{3,2,1,0:T(8,128)(2,1)S(1)} %bitcast.9), channel_id=1, source_target_pairs={{2,0},{4,2},{6,4},{0,6},{3,1},{5,3},{7,5},{1,7},{10,8},{12,10},{14... | collective-permute-start | bytes 1572872 | tf_op jit(solution)/shard_map/gather/ppermute | solution.py:332
  106.7 0.9 copy-start.2
  107.5 13.3 %collective-permute-start.8 = (bf16[16,2,32,128]{3,2,1,0:T(8,128)(2,1)}, bf16[16,2,32,128]{3,2,1,0:T(8,128)(2,1)S(1)}, u32[]{:S(2)}, u32[]{:S(2)}) collective-permute-start(bf16[16,2,32,128]{3,2,1,0:T(8,128)(2,1)} %slice.9), channel_id=1, source_target_pairs={{6,0},{0,2},{2,4},{4,6},{7,1},{1,3},{3,5},{5,7},{14,8},{8,10},{10,... | collective-permute-start | bytes 786440 | tf_op jit(solution)/shard_map/gather/ppermute | solution.py:334
  107.6 0.9 copy-start.4
  108.5 12.3 %collective-permute-start.6 = (bf16[16,2,32,128]{3,2,1,0:T(8,128)(2,1)}, bf16[16,2,32,128]{3,2,1,0:T(8,128)(2,1)}, u32[]{:S(2)}, u32[]{:S(2)}) collective-permute-start(bf16[16,2,32,128]{3,2,1,0:T(8,128)(2,1)} %slice.8), channel_id=1, source_target_pairs={{2,0},{4,2},{6,4},{0,6},{3,1},{5,3},{7,5},{1,7},{10,8},{12,10},{14... | collective-permute-start | bytes 786440 | tf_op jit(solution)/shard_map/gather/ppermute | solution.py:334
  111.0 1.0 copy-start.3
  112.1 1.0 copy-start.5
  113.1 1.6 %copy-start.6 = (bf16[4,32,2,32,128]{4,3,2,1,0:T(8,128)(2,1)S(1)}, bf16[4,32,2,32,128]{4,3,2,1,0:T(8,128)(2,1)}, u32[]{:S(2)}) copy-start(bf16[4,32,2,32,128]{4,3,2,1,0:T(8,128)(2,1)} %all-gather.2.cloned.1.call-done.refs_0_) | copy-start | bytes 6291460
Sparse Core Ops, SparseCore 0:
  65.2 33.0 all-gather.1

commit v5 on v3

--- a/solution.py
+++ b/solution.py
@@ -318,10 +318,10 @@
             far.append([lax.ppermute(above[:half], "inp", up), lax.ppermute(below[half:], "inp", down)])
         near += [[block], [above], [below]]
     with jax.named_scope("order"):
-        tables = picks([(turn, batch) for batch in range(BATCHES) for turn in (0, 1, 3)])
-        early = order_inputs(near, tables, chip_frames)
+        tables = picks([(turn, batch) for batch in range(BATCHES) for turn in (0, 1, 3)] + [(2, 0)])
+        early = order_inputs(near + far[:1], tables, chip_frames)
     with jax.named_scope("correlate"):
-        out = correlate(far, picks([(2, batch) for batch in range(BATCHES)]), early, scale, chip_frames, shape)
+        out = correlate(far[1:], picks([(2, batch) for batch in range(1, BATCHES)]), early, scale, chip_frames, shape)
     return out
 
 

time: 114 us -> 115 us (level)
  waiting for transfers between devices: 50.1 us -> 48.4 us
  Pallas kernels: 21.2 us -> 22.4 us
    pallas_call x1, Pallas kernels: 4.7 us -> 6.02 us  [order_inputs(): pl.pallas_call(functools.partial(order_kernel, counts, frames), out_shape...]
    unnamed x9 -> x7, local copies, waits for them, and re-layouts: 3.09 us -> 3.08 us
  transfers between devices with their start and end apart: 15 -> 15, of which waited for: 7 -> 7; matrix products, arithmetic and copies ran while one was open for 2% -> 2% of each run, Pallas kernels for 12% -> 13%
where the time goes in v5:
time: 115 us; the launch traced here: 114 us
  waiting for transfers between devices  48.4 us (42%)
  starting transfers between devices  38.1 us (33%)
  Pallas kernels  22.4 us (19%)
  local copies, waits for them, and re-layouts  3.31 us (3%)
  other arithmetic  1.66 us (1%)
    all_to_all x2, waiting for transfers between devices, local(): block = lax.all_to_all(spectra, TIME, 0, 0, tiled=True)  26.2 us
    all_to_all x2, starting transfers between devices, local(): block = lax.all_to_all(spectra, TIME, 0, 0, tiled=True)  12.4 us
    ppermute x2, starting transfers between devices, local(): lax.ppermute(o, TIME, route(-1, 0))  10.9 us
    pallas_call x2, Pallas kernels, filter_bank(): pl.pallas_call(functools.partial(filter_kernel, taps, frames), out_shape=...  9.21 us
    ppermute x2, waiting for transfers between devices, local(): lax.ppermute(block, 'inp', down)  8.15 us
    pallas_call x1, Pallas kernels, correlate(): pl.pallas_call(functools.partial(correlate_kernel, scale, counts, frames)...  6.49 us
    pallas_call x1, Pallas kernels, order_inputs(): pl.pallas_call(functools.partial(order_kernel, counts, frames), out_shape...  6.02 us
    ppermute x2, waiting for transfers between devices, local(): lax.ppermute(o, TIME, route(1, 0))  5.74 us
  transfers between devices with their start and end apart: 15, of which 7 were waited for; matrix products, arithmetic and copies ran while one was open for 2% of the time, Pallas kernels for 13%

profile of v5, /device:TPU:1, one launch (start us, length us, event | category | flops | bytes accessed | tf_op | source)
XLA Modules:
  0.0 114.1 jit_solution(1840758456526048138)
XLA Ops:
  0.0 1.2 %copy-done = bf16[4,2,256,256]{3,2,1,0:T(8,128)(2,1)S(1)} copy-done((bf16[4,2,256,256]{3,2,1,0:T(8,128)(2,1)S(1)}, bf16[4,2,256,256]{3,2,1,0:T(8,128)(2,1)}, u32[]{:S(2)}) %copy-start) | copy-done | bytes 1048600
  1.8 3.3 %collective-permute-start = (bf16[2,4,256,128]{3,2,1,0:T(8,128)(2,1)S(1)}, bf16[2,4,256,128]{3,2,1,0:T(8,128)(2,1)S(1)}, u32[]{:S(2)}, u32[]{:S(2)}) collective-permute-start(bf16[2,4,256,128]{3,2,1,0:T(8,128)(2,1)S(1)} %get-tuple-element.12), channel_id=1, source_target_pairs={{1,0},{0,1},{9,8},{8,9},{17,16},{16,17},{25,24},{24,25},{33,32},{3... | collective-permute-start | bytes 1572872 | tf_op jit(solution)/shard_map/halo/ppermute | solution.py:287
  5.1 0.8 copy.6
  5.9 1.0 copy-done.1
  7.1 6.1 %collective-permute-start.8 = (bf16[8,256,128]{2,1,0:T(8,128)(2,1)S(1)}, bf16[8,256,128]{2,1,0:T(8,128)(2,1)S(1)}, u32[]{:S(2)}, u32[]{:S(2)}) collective-permute-start(bf16[8,256,128]{2,1,0:T(8,128)(2,1)S(1)} %get-tuple-element.14.own), channel_id=1, source_target_pairs={{8,0},{9,1},{16,8},{17,9},{24,16},{25,17},{32,24},{33,25},{40,32},... | collective-permute-start | bytes 1572872 | tf_op jit(solution)/shard_map/halo/ppermute | solution.py:288
  14.2 4.8 %collective-permute-start.2 = (bf16[8,256,128]{2,1,0:T(8,128)(2,1)S(1)}, bf16[8,256,128]{2,1,0:T(8,128)(2,1)S(1)}, u32[]{:S(2)}, u32[]{:S(2)}) collective-permute-start(bf16[8,256,128]{2,1,0:T(8,128)(2,1)S(1)} %get-tuple-element.13.own), channel_id=1, source_target_pairs={{8,0},{9,1},{16,8},{17,9},{24,16},{25,17},{32,24},{33,25},{40,32},... | collective-permute-start | bytes 1572872 | tf_op jit(solution)/shard_map/halo/ppermute | solution.py:288
  19.0 5.6 %collective-permute-done.8.right = bf16[8,256,128]{2,1,0:T(8,128)(2,1)S(1)} collective-permute-done((bf16[8,256,128]{2,1,0:T(8,128)(2,1)S(1)}, bf16[8,256,128]{2,1,0:T(8,128)(2,1)S(1)}, u32[]{:S(2)}, u32[]{:S(2)}) %collective-permute-start.8) | collective-permute-done | bytes 524320 | tf_op jit(solution)/shard_map/halo/ppermute | solution.py:288
  24.5 5.2 %collective-permute-done.7.left = bf16[8,256,128]{2,1,0:T(8,128)(2,1)S(1)} collective-permute-done((bf16[8,256,128]{2,1,0:T(8,128)(2,1)S(1)}, bf16[8,256,128]{2,1,0:T(8,128)(2,1)S(1)}, u32[]{:S(2)}, u32[]{:S(2)}) %collective-permute-start.7) | collective-permute-done | bytes 524320 | tf_op jit(solution)/shard_map/halo/ppermute | solution.py:288
  29.7 4.6 %filter_bank.3 = bf16[64,32,128]{2,1,0:T(8,128)(2,1)} custom-call(s32[1]{0:T(128)} %bitcast.place, bf16[8,256,128]{2,1,0:T(8,128)(2,1)S(1)} %collective-permute-done.7.left, bf16[8,256,128]{2,1,0:T(8,128)(2,1)S(1)} %get-tuple-element.14.own, bf16[8,256,128]{2,1,0:T(8,128)(2,1)S(1)} %collective-permute-done.8.right, f32[256,16]{1,0:T(8,128)S(1)} %bitcast.14, ...), custom_call_target="tpu_custom_call" | custom-call | flops 20000000000 | bytes 1048576 | tf_op jit(solution)/shard_map/filter/filter_bank/pallas_call | solution.py:163
  34.3 6.0 %all-to-all-start.1 = ((bf16[64,32,128]{2,1,0:T(8,128)(2,1)}), bf16[64,32,128]{2,1,0:T(8,128)(2,1)S(1)}, u32[]{:S(2)}, u32[]{:S(2)}) async-start(bf16[64,32,128]{2,1,0:T(8,128)(2,1)} %filter_bank.3), calls=%async_computation.1 | async-start | bytes 1048576 | tf_op jit(solution)/shard_map/exchange/all_to_all | solution.py:313
  41.0 4.6 %filter_bank.2 = bf16[64,32,128]{2,1,0:T(8,128)(2,1)} custom-call(s32[1]{0:T(128)} %bitcast.place, bf16[8,256,128]{2,1,0:T(8,128)(2,1)S(1)} %collective-permute-done.1.left, bf16[8,256,128]{2,1,0:T(8,128)(2,1)S(1)} %get-tuple-element.13.own, bf16[8,256,128]{2,1,0:T(8,128)(2,1)S(1)} %collective-permute-done.2.right, f32[256,16]{1,0:T(8,128)S(1)} %bitcast.15, ...), custom_call_target="tpu_custom_call" | custom-call | flops 20000000000 | bytes 1048576 | tf_op jit(solution)/shard_map/filter/filter_bank/pallas_call | solution.py:163
  45.6 12.2 %all-to-all-done.1 = bf16[64,32,128]{2,1,0:T(8,128)(2,1)S(1)} async-done(((bf16[64,32,128]{2,1,0:T(8,128)(2,1)}), bf16[64,32,128]{2,1,0:T(8,128)(2,1)S(1)}, u32[]{:S(2)}, u32[]{:S(2)}) %all-to-all-start.1) | async-done | bytes 524320 | tf_op jit(solution)/shard_map/exchange/all_to_all | solution.py:313
  57.8 6.4 %all-to-all-start = ((bf16[64,32,128]{2,1,0:T(8,128)(2,1)}), bf16[64,32,128]{2,1,0:T(8,128)(2,1)S(1)}, u32[]{:S(2)}, u32[]{:S(2)}) async-start(bf16[64,32,128]{2,1,0:T(8,128)(2,1)} %filter_bank.2), calls=%async_computation | async-start | bytes 1048576 | tf_op jit(solution)/shard_map/exchange/all_to_all | solution.py:313
  64.4 1.4 %collective-permute-start.10 = (bf16[32,2,32,128]{3,2,1,0:T(8,128)(2,1)S(1)}, bf16[32,2,32,128]{3,2,1,0:T(8,128)(2,1)S(1)}, u32[]{:S(2)}, u32[]{:S(2)}) collective-permute-start(bf16[32,2,32,128]{3,2,1,0:T(8,128)(2,1)S(1)} %bitcast.8), channel_id=1, source_target_pairs={{6,0},{0,2},{2,4},{4,6},{7,1},{1,3},{3,5},{5,7},{14,8},{8,10},{10,... | collective-permute-start | bytes 1572872 | tf_op jit(solution)/shard_map/gather/ppermute | solution.py:316
  65.8 1.5 %collective-permute-start.9 = (bf16[32,2,32,128]{3,2,1,0:T(8,128)(2,1)S(1)}, bf16[32,2,32,128]{3,2,1,0:T(8,128)(2,1)S(1)}, u32[]{:S(2)}, u32[]{:S(2)}) collective-permute-start(bf16[32,2,32,128]{3,2,1,0:T(8,128)(2,1)S(1)} %bitcast.9), channel_id=1, source_target_pairs={{2,0},{4,2},{6,4},{0,6},{3,1},{5,3},{7,5},{1,7},{10,8},{12,10},{14... | collective-permute-start | bytes 1572872 | tf_op jit(solution)/shard_map/gather/ppermute | solution.py:316
  67.4 14.0 %all-to-all-done = bf16[64,32,128]{2,1,0:T(8,128)(2,1)S(1)} async-done(((bf16[64,32,128]{2,1,0:T(8,128)(2,1)}), bf16[64,32,128]{2,1,0:T(8,128)(2,1)S(1)}, u32[]{:S(2)}, u32[]{:S(2)}) %all-to-all-start) | async-done | bytes 524320 | tf_op jit(solution)/shard_map/exchange/all_to_all | solution.py:313
  81.4 1.3 %collective-permute-start.5 = (bf16[32,2,32,128]{3,2,1,0:T(8,128)(2,1)S(1)}, bf16[32,2,32,128]{3,2,1,0:T(8,128)(2,1)S(1)}, u32[]{:S(2)}, u32[]{:S(2)}) collective-permute-start(bf16[32,2,32,128]{3,2,1,0:T(8,128)(2,1)S(1)} %bitcast.11), channel_id=1, source_target_pairs={{6,0},{0,2},{2,4},{4,6},{7,1},{1,3},{3,5},{5,7},{14,8},{8,10},{10,... | collective-permute-start | bytes 1572872 | tf_op jit(solution)/shard_map/gather/ppermute | solution.py:316
  82.7 1.4 %collective-permute-start.3 = (bf16[32,2,32,128]{3,2,1,0:T(8,128)(2,1)S(1)}, bf16[32,2,32,128]{3,2,1,0:T(8,128)(2,1)S(1)}, u32[]{:S(2)}, u32[]{:S(2)}) collective-permute-start(bf16[32,2,32,128]{3,2,1,0:T(8,128)(2,1)S(1)} %bitcast.12), channel_id=1, source_target_pairs={{2,0},{4,2},{6,4},{0,6},{3,1},{5,3},{7,5},{1,7},{10,8},{12,10},{14... | collective-permute-start | bytes 1572872 | tf_op jit(solution)/shard_map/gather/ppermute | solution.py:316
  84.7 2.7 %collective-permute-start.11 = (bf16[16,2,32,128]{3,2,1,0:T(8,128)(2,1)S(1)}, bf16[16,2,32,128]{3,2,1,0:T(8,128)(2,1)S(1)}, u32[]{:S(2)}, u32[]{:S(2)}) collective-permute-start(bf16[16,2,32,128]{3,2,1,0:T(8,128)(2,1)S(1)} %slice.18), channel_id=1, source_target_pairs={{2,0},{4,2},{6,4},{0,6},{3,1},{5,3},{7,5},{1,7},{10,8},{12,10},{14... | collective-permute-start | bytes 786440 | tf_op jit(solution)/shard_map/gather/ppermute | solution.py:318
  87.8 8.1 %collective-permute-done.5.refs_5_ = bf16[32,2,32,128]{3,2,1,0:T(8,128)(2,1)S(1)} collective-permute-done((bf16[32,2,32,128]{3,2,1,0:T(8,128)(2,1)S(1)}, bf16[32,2,32,128]{3,2,1,0:T(8,128)(2,1)S(1)}, u32[]{:S(2)}, u32[]{:S(2)}) %collective-permute-start.5) | collective-permute-done | bytes 524320 | tf_op jit(solution)/shard_map/gather/ppermute | solution.py:316
  96.1 2.7 %collective-permute-start.4 = (bf16[16,2,32,128]{3,2,1,0:T(8,128)(2,1)S(1)}, bf16[16,2,32,128]{3,2,1,0:T(8,128)(2,1)S(1)}, u32[]{:S(2)}, u32[]{:S(2)}) collective-permute-start(bf16[16,2,32,128]{3,2,1,0:T(8,128)(2,1)S(1)} %slice.16), channel_id=1, source_target_pairs={{2,0},{4,2},{6,4},{0,6},{3,1},{5,3},{7,5},{1,7},{10,8},{12,10},{14... | collective-permute-start | bytes 786440 | tf_op jit(solution)/shard_map/gather/ppermute | solution.py:318
  98.9 2.7 %collective-permute-done.12.refs_7_ = bf16[16,2,32,128]{3,2,1,0:T(8,128)(2,1)S(1)} collective-permute-done((bf16[16,2,32,128]{3,2,1,0:T(8,128)(2,1)S(1)}, bf16[16,2,32,128]{3,2,1,0:T(8,128)(2,1)S(1)}, u32[]{:S(2)}, u32[]{:S(2)}) %collective-permute-start.12) | collective-permute-done | bytes 262176 | tf_op jit(solution)/shard_map/gather/ppermute | solution.py:318
  101.6 6.0 %order_inputs.1 = (bf16[4,512,1024]{2,1,0:T(8,128)(2,1)S(1)}, bf16[4,512,512]{2,1,0:T(8,128)(2,1)S(1)}) custom-call(bf16[32,2,32,128]{3,2,1,0:T(8,128)(2,1)S(1)} %bitcast.10, bf16[32,2,32,128]{3,2,1,0:T(8,128)(2,1)S(1)} %collective-permute-done.9.refs_1_, bf16[32,2,32,128]{3,2,1,0:T(8,128)(2,1)S(1)} %collective-permute-done.10.refs_2_, ...), custom_call_target="tpu_custom_call" | custom-call | flops 4697620480 | bytes 1048576 | tf_op jit(solution)/shard_map/order/order_inputs/pallas_call | solution.py:229
  107.6 6.5 %correlate.1 = f32[4,2,256,1024]{3,2,1,0:T(8,128)} custom-call(bf16[16,2,32,128]{3,2,1,0:T(8,128)(2,1)S(1)} %collective-permute-done.4.refs_0_, bf16[16,2,32,128]{3,2,1,0:T(8,128)(2,1)S(1)} %collective-permute-done.6.refs_1_, bf16[128,1024]{1,0:T(8,128)(2,1)S(1)} %compare_convert_fusion.2.refs_2_, bf16[128,256]{1,0:T(8,128)(2,1)S(1)} %compare_convert_fusion.3.refs_3_, ...), custom_call_target="tpu_custom_call" | custom-call | tf_op jit(solution)/shard_map/correlate/correlate/pallas_call | solution.py:261
  (42 shorter events, 3.5 us)
Async XLA Ops:
  0.0 1.2 %copy-start = (bf16[4,2,256,256]{3,2,1,0:T(8,128)(2,1)S(1)}, bf16[4,2,256,256]{3,2,1,0:T(8,128)(2,1)}, u32[]{:S(2)}) copy-start(bf16[4,2,256,256]{3,2,1,0:T(8,128)(2,1)} %voltages.1) | copy-start | bytes 3145732
  1.8 5.3 %collective-permute-start = (bf16[2,4,256,128]{3,2,1,0:T(8,128)(2,1)S(1)}, bf16[2,4,256,128]{3,2,1,0:T(8,128)(2,1)S(1)}, u32[]{:S(2)}, u32[]{:S(2)}) collective-permute-start(bf16[2,4,256,128]{3,2,1,0:T(8,128)(2,1)S(1)} %get-tuple-element.12), channel_id=1, source_target_pairs={{1,0},{0,1},{9,8},{8,9},{17,16},{16,17},{25,24},{24,25},{33,32},{3... | collective-permute-start | bytes 1572872 | tf_op jit(solution)/shard_map/halo/ppermute | solution.py:287
  5.9 1.0 copy-start.1
  7.1 17.4 %collective-permute-start.8 = (bf16[8,256,128]{2,1,0:T(8,128)(2,1)S(1)}, bf16[8,256,128]{2,1,0:T(8,128)(2,1)S(1)}, u32[]{:S(2)}, u32[]{:S(2)}) collective-permute-start(bf16[8,256,128]{2,1,0:T(8,128)(2,1)S(1)} %get-tuple-element.14.own), channel_id=1, source_target_pairs={{8,0},{9,1},{16,8},{17,9},{24,16},{25,17},{32,24},{33,25},{40,32},... | collective-permute-start | bytes 1572872 | tf_op jit(solution)/shard_map/halo/ppermute | solution.py:288
  13.3 16.5 %collective-permute-start.7 = (bf16[8,256,128]{2,1,0:T(8,128)(2,1)S(1)}, bf16[8,256,128]{2,1,0:T(8,128)(2,1)S(1)}, u32[]{:S(2)}, u32[]{:S(2)}) collective-permute-start(bf16[8,256,128]{2,1,0:T(8,128)(2,1)S(1)} %get-tuple-element.14.own), channel_id=1, source_target_pairs={{248,0},{249,1},{0,8},{1,9},{8,16},{9,17},{16,24},{17,25},{24,32},... | collective-permute-start | bytes 1572872 | tf_op jit(solution)/shard_map/halo/ppermute | solution.py:288
  14.2 26.2 %collective-permute-start.2 = (bf16[8,256,128]{2,1,0:T(8,128)(2,1)S(1)}, bf16[8,256,128]{2,1,0:T(8,128)(2,1)S(1)}, u32[]{:S(2)}, u32[]{:S(2)}) collective-permute-start(bf16[8,256,128]{2,1,0:T(8,128)(2,1)S(1)} %get-tuple-element.13.own), channel_id=1, source_target_pairs={{8,0},{9,1},{16,8},{17,9},{24,16},{25,17},{32,24},{33,25},{40,32},... | collective-permute-start | bytes 1572872 | tf_op jit(solution)/shard_map/halo/ppermute | solution.py:288
  19.0 22.0 %collective-permute-start.1 = (bf16[8,256,128]{2,1,0:T(8,128)(2,1)S(1)}, bf16[8,256,128]{2,1,0:T(8,128)(2,1)S(1)}, u32[]{:S(2)}, u32[]{:S(2)}) collective-permute-start(bf16[8,256,128]{2,1,0:T(8,128)(2,1)S(1)} %get-tuple-element.13.own), channel_id=1, source_target_pairs={{248,0},{249,1},{0,8},{1,9},{8,16},{9,17},{16,24},{17,25},{24,32},... | collective-permute-start | bytes 1572872 | tf_op jit(solution)/shard_map/halo/ppermute | solution.py:288
  34.3 23.4 %all-to-all-start.1 = ((bf16[64,32,128]{2,1,0:T(8,128)(2,1)}), bf16[64,32,128]{2,1,0:T(8,128)(2,1)S(1)}, u32[]{:S(2)}, u32[]{:S(2)}) async-start(bf16[64,32,128]{2,1,0:T(8,128)(2,1)} %filter_bank.3), calls=%async_computation.1 | async-start | bytes 1048576 | tf_op jit(solution)/shard_map/exchange/all_to_all | solution.py:313
  40.4 23.8 %copy-start.2 = (s32[1024]{0:T(1024)S(1)}, s32[1024]{0:T(1024)}, u32[]{:S(2)}) copy-start(s32[1024]{0:T(1024)} %param.7) | copy-start | bytes 12292
  57.8 23.7 %all-to-all-start = ((bf16[64,32,128]{2,1,0:T(8,128)(2,1)}), bf16[64,32,128]{2,1,0:T(8,128)(2,1)S(1)}, u32[]{:S(2)}, u32[]{:S(2)}) async-start(bf16[64,32,128]{2,1,0:T(8,128)(2,1)} %filter_bank.2), calls=%async_computation | async-start | bytes 1048576 | tf_op jit(solution)/shard_map/exchange/all_to_all | solution.py:313
  64.4 20.0 %collective-permute-start.10 = (bf16[32,2,32,128]{3,2,1,0:T(8,128)(2,1)S(1)}, bf16[32,2,32,128]{3,2,1,0:T(8,128)(2,1)S(1)}, u32[]{:S(2)}, u32[]{:S(2)}) collective-permute-start(bf16[32,2,32,128]{3,2,1,0:T(8,128)(2,1)S(1)} %bitcast.8), channel_id=1, source_target_pairs={{6,0},{0,2},{2,4},{4,6},{7,1},{1,3},{3,5},{5,7},{14,8},{8,10},{10,... | collective-permute-start | bytes 1572872 | tf_op jit(solution)/shard_map/gather/ppermute | solution.py:316
  65.8 18.9 %collective-permute-start.9 = (bf16[32,2,32,128]{3,2,1,0:T(8,128)(2,1)S(1)}, bf16[32,2,32,128]{3,2,1,0:T(8,128)(2,1)S(1)}, u32[]{:S(2)}, u32[]{:S(2)}) collective-permute-start(bf16[32,2,32,128]{3,2,1,0:T(8,128)(2,1)S(1)} %bitcast.9), channel_id=1, source_target_pairs={{2,0},{4,2},{6,4},{0,6},{3,1},{5,3},{7,5},{1,7},{10,8},{12,10},{14... | collective-permute-start | bytes 1572872 | tf_op jit(solution)/shard_map/gather/ppermute | solution.py:316
  81.4 14.5 %collective-permute-start.5 = (bf16[32,2,32,128]{3,2,1,0:T(8,128)(2,1)S(1)}, bf16[32,2,32,128]{3,2,1,0:T(8,128)(2,1)S(1)}, u32[]{:S(2)}, u32[]{:S(2)}) collective-permute-start(bf16[32,2,32,128]{3,2,1,0:T(8,128)(2,1)S(1)} %bitcast.11), channel_id=1, source_target_pairs={{6,0},{0,2},{2,4},{4,6},{7,1},{1,3},{3,5},{5,7},{14,8},{8,10},{10,... | collective-permute-start | bytes 1572872 | tf_op jit(solution)/shard_map/gather/ppermute | solution.py:316
  82.7 13.4 %collective-permute-start.3 = (bf16[32,2,32,128]{3,2,1,0:T(8,128)(2,1)S(1)}, bf16[32,2,32,128]{3,2,1,0:T(8,128)(2,1)S(1)}, u32[]{:S(2)}, u32[]{:S(2)}) collective-permute-start(bf16[32,2,32,128]{3,2,1,0:T(8,128)(2,1)S(1)} %bitcast.12), channel_id=1, source_target_pairs={{2,0},{4,2},{6,4},{0,6},{3,1},{5,3},{7,5},{1,7},{10,8},{12,10},{14... | collective-permute-start | bytes 1572872 | tf_op jit(solution)/shard_map/gather/ppermute | solution.py:316
  84.4 17.2 %collective-permute-start.12 = (bf16[16,2,32,128]{3,2,1,0:T(8,128)(2,1)S(1)}, bf16[16,2,32,128]{3,2,1,0:T(8,128)(2,1)S(1)}, u32[]{:S(2)}, u32[]{:S(2)}) collective-permute-start(bf16[16,2,32,128]{3,2,1,0:T(8,128)(2,1)S(1)} %slice.19), channel_id=1, source_target_pairs={{6,0},{0,2},{2,4},{4,6},{7,1},{1,3},{3,5},{5,7},{14,8},{8,10},{10,... | collective-permute-start | bytes 786440 | tf_op jit(solution)/shard_map/gather/ppermute | solution.py:318
  84.7 16.9 %collective-permute-start.11 = (bf16[16,2,32,128]{3,2,1,0:T(8,128)(2,1)S(1)}, bf16[16,2,32,128]{3,2,1,0:T(8,128)(2,1)S(1)}, u32[]{:S(2)}, u32[]{:S(2)}) collective-permute-start(bf16[16,2,32,128]{3,2,1,0:T(8,128)(2,1)S(1)} %slice.18), channel_id=1, source_target_pairs={{2,0},{4,2},{6,4},{0,6},{3,1},{5,3},{7,5},{1,7},{10,8},{12,10},{14... | collective-permute-start | bytes 786440 | tf_op jit(solution)/shard_map/gather/ppermute | solution.py:318
  96.0 11.6 %collective-permute-start.6 = (bf16[16,2,32,128]{3,2,1,0:T(8,128)(2,1)S(1)}, bf16[16,2,32,128]{3,2,1,0:T(8,128)(2,1)S(1)}, u32[]{:S(2)}, u32[]{:S(2)}) collective-permute-start(bf16[16,2,32,128]{3,2,1,0:T(8,128)(2,1)S(1)} %slice.17), channel_id=1, source_target_pairs={{6,0},{0,2},{2,4},{4,6},{7,1},{1,3},{3,5},{5,7},{14,8},{8,10},{10,... | collective-permute-start | bytes 786440 | tf_op jit(solution)/shard_map/gather/ppermute | solution.py:318
  96.1 11.5 %collective-permute-start.4 = (bf16[16,2,32,128]{3,2,1,0:T(8,128)(2,1)S(1)}, bf16[16,2,32,128]{3,2,1,0:T(8,128)(2,1)S(1)}, u32[]{:S(2)}, u32[]{:S(2)}) collective-permute-start(bf16[16,2,32,128]{3,2,1,0:T(8,128)(2,1)S(1)} %slice.16), channel_id=1, source_target_pairs={{2,0},{4,2},{6,4},{0,6},{3,1},{5,3},{7,5},{1,7},{10,8},{12,10},{14... | collective-permute-start | bytes 786440 | tf_op jit(solution)/shard_map/gather/ppermute | solution.py:318
